TPU v7x, 32 devices: a whole 2x2x4 slice. The times are simulated.
32 devices in a mesh: strip: 8 (over y, x, core), dict: 4 (over z).
Axes of the slice: x: 2, y: 2, z: 4, core: 2. Of those that a mesh axis runs over, the one named last changes fastest.
Arguments:
- patterns: bfloat16 [3600, 64, 512], P(None, 'strip', 'dict'), may hold values from -100 to 160
- scan_mask: int32 [64, 512], P('strip', 'dict'), may hold values 0 or 1
- neighbour_mask: int32 [8, 64, 512], P(None, 'strip', 'dict'), may hold values 0 or 1
- dictionary: bfloat16 [2, 512, 3600], P(None, ('strip', 'dict')), may hold values from -160 to 160
Outputs:
- top_scores: float32 [2, 4, 64, 512], P(None, None, 'strip', 'dict')
All inputs are finite; a program needn't handle non-finite values. No bound on the sum of `scan_mask` or of `neighbour_mask` on one device may be relied on, other than what follows from the above.
Results may differ from a plain program's by a relative error of at most 0.00081.
Values may be sent and summed in bfloat16 or wider, within the bound.
No kernel may reach another device: no remote copies, remote signals or barrier semaphores. Data moves between devices by JAX's collectives and lax.ppermute only.
A program may use at most 192 MiB of HBM per device.

v0:
```python
import functools

import jax
import jax.numpy as jnp
import ml_dtypes
import numpy as np
from jax import lax
from jax.experimental import pallas as pl
from jax.experimental.pallas import tpu as pltpu
from jax.sharding import PartitionSpec as P

PH = 60
TOP = 4
QUAD = 4
GROUPS = PH // QUAD
TILE = QUAD * QUAD
CHUNK = GROUPS * TILE
DEPTH = 256
LANES = 128
SIDES = 32

epsilon = 1e-05
nlpar_scale = 2.0
MIB = 1 << 20


def blur_matrix():
    at = np.arange(PH, dtype=np.float32)
    spread_px = np.float32(PH / 8.0)
    gap = at[:, None] - at[None, :]
    profile = np.exp(-(gap * gap) / (np.float32(2.0) * spread_px * spread_px))
    profile = profile / profile.sum(axis=1, keepdims=True)
    return profile.astype(ml_dtypes.bfloat16).astype(np.float32)


def pass_matrices():
    kernel = blur_matrix()
    index = np.arange(CHUNK)
    quad, row, col = index // TILE, (index // QUAD) % QUAD, index % QUAD
    along = quad * QUAD + col
    columns = kernel[along[:, None], along[None, :]] * (row[:, None] == row[None, :])
    down = quad * QUAD + row
    rows = kernel[down[:, None], down[None, :]] * (col[:, None] == col[None, :])
    natural = row * PH + along
    order = (index[:, None] == natural[None, :]).astype(np.float32)
    out = np.zeros((3, CHUNK, DEPTH), np.float32)
    out[0, :, :CHUNK], out[1, :, :CHUNK], out[2, :, :CHUNK] = columns, rows, order
    return out.astype(ml_dtypes.bfloat16)


def tiles_of(pieces):
    return jnp.concatenate(pieces + [pieces[-1]], axis=0)


def standardize_kernel(x_hbm, mask_ref, mat_ref, s_ref, raw, xq, half, corr, sq, sems):
    pair = pl.program_id(0)

    @pl.when(pair == 0)
    def _():
        def fetch(g):
            return pltpu.make_async_copy(x_hbm.at[pl.ds(g * CHUNK, CHUNK)], raw.at[g], sems.at[g])

        for g in range(GROUPS):
            fetch(g).start()
        mask = mask_ref[...].astype(jnp.bfloat16)[None]

        for g in range(GROUPS):
            fetch(g).wait()
            for quad in range(GROUPS):
                piece = jnp.concatenate(
                    [raw[g, pl.ds(row * PH + quad * QUAD, QUAD)] for row in range(QUAD)], axis=0
                )
                xq[:, quad, pl.ds(g * TILE, TILE), :] = jnp.swapaxes(piece * mask, 0, 1)

    r0 = pair * 2

    def both(quad, rows):
        return jnp.concatenate([xq[r0, quad, rows, :], xq[r0 + 1, quad, rows, :]], axis=1)

    for g in range(GROUPS):
        rhs = tiles_of([both(quad, pl.ds(g * TILE, TILE)) for quad in range(GROUPS)])
        out = jnp.dot(mat_ref[0], rhs, preferred_element_type=jnp.float32)
        half[g] = out.astype(jnp.bfloat16)

    total = jnp.zeros((8, 2 * LANES), jnp.float32)
    squares = jnp.zeros((8, 2 * LANES), jnp.float32)
    for quad in range(GROUPS):
        rhs = tiles_of([half[g, pl.ds(quad * TILE, TILE), :] for g in range(GROUPS)])
        background = jnp.dot(mat_ref[1], rhs, preferred_element_type=jnp.float32)
        corrected = both(quad, slice(None)).astype(jnp.float32) - background
        corr[quad] = corrected
        folded = corrected.reshape(CHUNK // 8, 8, 2 * LANES)
        total = total + jnp.sum(folded, axis=0)
        squares = squares + jnp.sum(folded * folded, axis=0)
    pixels = GROUPS * CHUNK
    mean = jnp.sum(total, axis=0, keepdims=True) / pixels
    variance = jnp.sum(squares, axis=0, keepdims=True) / pixels - mean * mean
    scale = 1.0 / jnp.sqrt(jnp.maximum(variance, 0.0) + epsilon)
    for quad in range(GROUPS):
        sq[quad] = ((corr[quad] - mean) * scale).astype(jnp.bfloat16)
    for g in range(GROUPS):
        rhs = tiles_of([sq[quad, pl.ds(g * TILE, TILE), :] for quad in range(GROUPS)])
        out = jnp.dot(mat_ref[2], rhs, preferred_element_type=jnp.float32).astype(jnp.bfloat16)
        s_ref[0, pl.ds(g * CHUNK, CHUNK), :] = out[:, :LANES]
        s_ref[1, pl.ds(g * CHUNK, CHUNK), :] = out[:, LANES:]


def standardize(patterns, scan_mask):
    pixels, rows, cols = patterns.shape
    return pl.pallas_call(
        standardize_kernel,
        grid=(rows // 2,),
        in_specs=[
            pl.BlockSpec(memory_space=pl.ANY),
            pl.BlockSpec((rows, cols), lambda i: (0, 0)),
            pl.BlockSpec((3, CHUNK, DEPTH), lambda i: (0, 0, 0)),
        ],
        out_specs=pl.BlockSpec((2, pixels, cols), lambda i: (i, 0, 0)),
        out_shape=jax.ShapeDtypeStruct((rows, pixels, cols), jnp.bfloat16),
        scratch_shapes=[
            pltpu.VMEM((GROUPS, CHUNK, rows, cols), jnp.bfloat16),
            pltpu.VMEM((rows, GROUPS, CHUNK, cols), jnp.bfloat16),
            pltpu.VMEM((GROUPS, CHUNK, 2 * cols), jnp.bfloat16),
            pltpu.VMEM((GROUPS, CHUNK, 2 * cols), jnp.float32),
            pltpu.VMEM((GROUPS, CHUNK, 2 * cols), jnp.bfloat16),
            pltpu.SemaphoreType.DMA((GROUPS,)),
        ],
        compiler_params=pltpu.CompilerParams(vmem_limit_bytes=48 * MIB),
        cost_estimate=pl.CostEstimate(
            flops=6_000_000_000, bytes_accessed=15_000_000, transcendentals=0
        ),
        name="standardize",
    )(patterns, scan_mask, jnp.asarray(pass_matrices()))


def edges_kernel(s_ref, o_ref):
    rows = s_ref.shape[0]
    at_row = lax.broadcasted_iota(jnp.int32, (2 * rows, 2 * LANES), 0)
    at_lane = lax.broadcasted_iota(jnp.int32, (2 * rows, 2 * LANES), 1)
    for g in range(GROUPS):
        span = pl.ds(g * CHUNK, CHUNK)
        out = jnp.zeros((2 * rows, CHUNK), jnp.float32)
        for r in range(0, rows, 2):
            wanted = jnp.where(at_row < rows, 0, LANES - 1)
            row = jnp.where(at_row < rows, at_row, at_row - rows)
            pick = (at_lane == wanted + (row - r) * LANES).astype(jnp.bfloat16)
            block = jnp.concatenate([s_ref[r, span, :], s_ref[r + 1, span, :]], axis=1)
            out = out + lax.dot_general(
                pick, block, (((1,), (1,)), ((), ())), preferred_element_type=jnp.float32
            )
        o_ref[:, g * CHUNK : (g + 1) * CHUNK] = out.astype(jnp.bfloat16)


def edges(standard):
    rows, pixels, _ = standard.shape
    return pl.pallas_call(
        edges_kernel,
        out_shape=jax.ShapeDtypeStruct((2 * rows, pixels), jnp.bfloat16),
        compiler_params=pltpu.CompilerParams(vmem_limit_bytes=48 * MIB),
        name="edges",
    )(standard)


def diagonals(product, at_sub, at_lane):
    return [
        jnp.sum(jnp.where(at_sub == at_lane + d, product, 0.0), axis=0, keepdims=True)
        for d in (-1, 0, 1)
    ]


def average_kernel(s_ref, top_ref, bottom_ref, side_ref, usable_ref, a_ref, inv_ref, sides, weights):
    rows, pixels, cols = s_ref.shape
    f32 = jnp.float32
    at_sub = lax.broadcasted_iota(jnp.int32, (cols, cols), 0)
    at_lane = lax.broadcasted_iota(jnp.int32, (cols, cols), 1)
    lane = lax.broadcasted_iota(jnp.int32, (1, cols), 1)

    def row_ref(r):
        return top_ref if r < 0 else bottom_ref if r >= rows else s_ref.at[r]

    side32 = side_ref[...].astype(f32)
    side_norm = jnp.sum(side32 * side32, axis=1, keepdims=True)
    pad = jnp.concatenate([side32, jnp.zeros((cols - SIDES, pixels), f32)], axis=0)
    for start in range(0, pixels, LANES):
        width = min(LANES, pixels - start)
        sides[pl.ds(start, width), :] = pad[:, start : start + width].T.astype(jnp.bfloat16)

    norm, to_next, to_self, to_side = {}, {}, {}, {}
    for r in range(-1, rows + 1):
        here = row_ref(r)[...]
        here32 = here.astype(f32)
        norm[r] = jnp.sum(here32 * here32, axis=0, keepdims=True)
        if r < rows:
            nxt = row_ref(r + 1)[...]
            both = jnp.concatenate([here, nxt], axis=1)
            product = lax.dot_general(here, both, (((0,), (0,)), ((), ())), preferred_element_type=f32)
            to_next[r] = diagonals(product[:, cols:], at_sub, at_lane)
            to_self[r] = diagonals(product[:, :cols], at_sub, at_lane)
        if 0 <= r < rows:
            to_side[r] = jnp.dot(side_ref[...], here, preferred_element_type=f32)

    def shifted(vector, dc):
        if dc == 0:
            return vector
        return pltpu.roll(vector, (-dc) % cols, 1)

    for r in range(rows):
        weight = {}
        slot = 0
        total = jnp.ones((1, cols), f32)
        for dr in (-1, 0, 1):
            for dc in (-1, 0, 1):
                if dr == 0 and dc == 0:
                    continue
                if dr == -1:
                    dot = to_next[r - 1][dc + 1]
                elif dr == 1:
                    dot = shifted(to_next[r][-dc + 1], dc)
                else:
                    dot = to_self[r][0] if dc == -1 else shifted(to_self[r][0], 1)
                other = shifted(norm[r + dr], dc)
                if dc != 0:
                    k = r + dr + 1 + (0 if dc < 0 else 16)
                    end = 0 if dc < 0 else cols - 1
                    dot = jnp.where(lane == end, to_side[r][k : k + 1, :], dot)
                    other = jnp.where(lane == end, side_norm[k : k + 1, :], other)
                distance = jnp.maximum(norm[r] + other - 2.0 * dot, 0.0) / pixels
                weight[dr, dc] = usable_ref[slot, pl.ds(r, 1), :] * jnp.exp(-distance / nlpar_scale)
                total = total + weight[dr, dc]
                slot += 1
        for dr in (-1, 0, 1):
            block = jnp.zeros((cols, cols), f32)
            for dc in (-1, 0, 1):
                w = jnp.ones((1, cols), f32) if dr == 0 and dc == 0 else weight[dr, dc]
                block = jnp.where(at_sub == at_lane + dc, w, block)
            weights[r, dr + 1] = block
        block = jnp.zeros((cols, cols), f32)
        for dr in (-1, 0, 1):
            for dc in (-1, 1):
                k = r + dr + 1 + (0 if dc < 0 else 16)
                end = 0 if dc < 0 else cols - 1
                block = jnp.where((at_sub == k) & (at_lane == end), weight[dr, dc], block)
        weights[r, 3] = block

        full = weights[r].reshape(4 * cols, cols)
        high = full.astype(jnp.bfloat16)
        low = (full - high.astype(f32)).astype(jnp.bfloat16)
        split = jnp.concatenate([high, low], axis=1)
        inverse = 1.0 / total
        squares = jnp.zeros((8, cols), f32)
        for g in range(GROUPS):
            span = pl.ds(g * CHUNK, CHUNK)
            lhs = jnp.concatenate(
                [row_ref(r - 1)[span, :], row_ref(r)[span, :], row_ref(r + 1)[span, :], sides[span, :]],
                axis=1,
            )
            out = jnp.dot(lhs, split, preferred_element_type=f32)
            mean = ((out[:, :cols] + out[:, cols:]) * inverse).astype(jnp.bfloat16)
            a_ref[r, span, :] = mean
            mean32 = mean.astype(f32).reshape(CHUNK // 8, 8, cols)
            squares = squares + jnp.sum(mean32 * mean32, axis=0)
        energy = jnp.sum(squares, axis=0, keepdims=True) / pixels
        inv_ref[pl.ds(r, 1), :] = 1.0 / jnp.sqrt(energy + epsilon)


def average(standard, top, bottom, side, usable):
    rows, pixels, cols = standard.shape
    return pl.pallas_call(
        average_kernel,
        out_shape=(
            jax.ShapeDtypeStruct((rows, pixels, cols), jnp.bfloat16),
            jax.ShapeDtypeStruct((rows, cols), jnp.float32),
        ),
        scratch_shapes=[
            pltpu.VMEM((pixels, cols), jnp.bfloat16),
            pltpu.VMEM((rows, 4, cols, cols), jnp.float32),
        ],
        compiler_params=pltpu.CompilerParams(vmem_limit_bytes=48 * MIB),
        cost_estimate=pl.CostEstimate(
            flops=12_000_000_000, bytes_accessed=17_000_000, transcendentals=0
        ),
        name="average",
    )(standard, top, bottom, side, usable)


def insert(best, new):
    kept = []
    for slot, held in enumerate(best):
        kept.append(jnp.maximum(held, new))
        if slot < len(best) - 1:
            new = jnp.minimum(held, new)
    return kept


def merge_sublanes(best):
    for shift in (4, 2, 1):
        other = [pltpu.roll(b, shift, 0) for b in best]
        m = [jnp.maximum(best[i], other[3 - i]) for i in range(4)]
        a, c = jnp.maximum(m[0], m[2]), jnp.minimum(m[0], m[2])
        b, d = jnp.maximum(m[1], m[3]), jnp.minimum(m[1], m[3])
        best = [jnp.maximum(a, b), jnp.minimum(a, b), jnp.maximum(c, d), jnp.minimum(c, d)]
    return best


def score_kernel(d_ref, a_ref, inv_ref, o_ref, best):
    chunk, chunks = pl.program_id(1), pl.num_programs(1)
    rows, pixels, cols = a_ref.shape
    f32 = jnp.float32

    @pl.when(chunk == 0)
    def _():
        best[...] = jnp.full(best.shape, -jnp.inf, f32)

    entries = d_ref[0]
    entries32 = entries.astype(f32)
    energy = jnp.sum(entries32 * entries32, axis=1, keepdims=True) / pixels
    inv_entry = 1.0 / jnp.sqrt(energy + epsilon)
    for r in range(0, rows, 2):
        block = jnp.concatenate([a_ref[r], a_ref[r + 1]], axis=1)
        products = jnp.dot(entries, block, preferred_element_type=f32)
        scores = products / pixels * inv_entry
        for half in range(2):
            held = [best[j, r + half] for j in range(TOP)]
            for e in range(0, entries.shape[0], 8):
                held = insert(held, scores[e : e + 8, half * cols : (half + 1) * cols])
            for j in range(TOP):
                best[j, r + half] = held[j]

    @pl.when(chunk == chunks - 1)
    def _():
        for r in range(rows):
            held = merge_sublanes([best[j, r] for j in range(TOP)])
            for j in range(TOP):
                o_ref[0, j, pl.ds(r, 1), :] = held[j][:1] * inv_ref[pl.ds(r, 1), :]


def score(dictionary, averaged, inv_pattern, size=128):
    panels, entries, pixels = dictionary.shape
    rows, _, cols = averaged.shape
    return pl.pallas_call(
        score_kernel,
        grid=(panels, entries // size),
        in_specs=[
            pl.BlockSpec((1, size, pixels), lambda k, i: (k, i, 0)),
            pl.BlockSpec((rows, pixels, cols), lambda k, i: (0, 0, 0), pipeline_mode=pl.Buffered(1)),
            pl.BlockSpec((rows, cols), lambda k, i: (0, 0)),
        ],
        out_specs=pl.BlockSpec((1, TOP, rows, cols), lambda k, i: (k, 0, 0, 0)),
        out_shape=jax.ShapeDtypeStruct((panels, TOP, rows, cols), jnp.float32),
        scratch_shapes=[pltpu.VMEM((TOP, rows, 8, cols), jnp.float32)],
        compiler_params=pltpu.CompilerParams(vmem_limit_bytes=48 * MIB),
        cost_estimate=pl.CostEstimate(
            flops=7_500_000_000, bytes_accessed=15_000_000, transcendentals=0
        ),
        name="score",
    )(dictionary, averaged, inv_pattern)


def from_low(x, axis):
    count = lax.axis_size(axis)
    return lax.ppermute(x, axis, [(i, i + 1) for i in range(count - 1)])


def from_high(x, axis):
    count = lax.axis_size(axis)
    return lax.ppermute(x, axis, [(i + 1, i) for i in range(count - 1)])


def usable_neighbours(neighbour_mask):
    _, rows, cols = neighbour_mask.shape
    row_at = lax.axis_index("strip") * rows + jnp.arange(rows, dtype=jnp.int32)
    col_at = lax.axis_index("dict") * cols + jnp.arange(cols, dtype=jnp.int32)
    all_rows = rows * lax.axis_size("strip")
    all_cols = cols * lax.axis_size("dict")
    inside = []
    for dr in (-1, 0, 1):
        for dc in (-1, 0, 1):
            if dr == 0 and dc == 0:
                continue
            row_ok = (row_at + dr >= 0) & (row_at + dr < all_rows)
            col_ok = (col_at + dc >= 0) & (col_at + dc < all_cols)
            inside.append(row_ok[:, None] & col_ok[None, :])
    return (jnp.stack(inside) & (neighbour_mask == 1)).astype(jnp.float32)


def on_device(patterns, scan_mask, neighbour_mask, dictionary):
    rows = patterns.shape[1]
    portion = lax.all_gather(dictionary, ("strip", "dict"), axis=1, tiled=True)
    usable = usable_neighbours(neighbour_mask)
    standard = standardize(patterns, scan_mask)
    top = from_low(standard[rows - 1], "strip")
    bottom = from_high(standard[0], "strip")
    own = edges(standard)
    left = from_low(own, "dict")[rows:]
    right = from_high(own, "dict")[:rows]
    ends = jnp.concatenate([left, right], axis=0)
    above = from_low(ends, "strip")
    below = from_high(ends, "strip")
    blank = jnp.zeros((16 - rows - 2, own.shape[1]), own.dtype)
    side = jnp.concatenate(
        [
            above[rows - 1 : rows], left, below[:1], blank,
            above[2 * rows - 1 :], right, below[rows : rows + 1], blank,
        ],
        axis=0,
    )
    averaged, inv_pattern = average(standard, top, bottom, side, usable)
    return score(portion, averaged, inv_pattern)


def solution(mesh):
    in_specs = (
        P(None, "strip", "dict"),
        P("strip", "dict"),
        P(None, "strip", "dict"),
        P(None, ("strip", "dict"), None),
    )
    out_specs = P(None, None, "strip", "dict")
    return jax.shard_map(
        on_device, mesh=mesh, in_specs=in_specs, out_specs=out_specs, check_vma=False
    )
```

profile of v0, /device:TPU:1, one launch (start us, length us, event | category | flops | bytes accessed | tf_op | source)
XLA Modules:
  0.0 117.5 jit_solution(5221811865225395411)
XLA Ops:
  6.5 0.7 all-gather.2.cloned.1.call-update
  7.3 0.7 copy-done
  7.9 1.0 copy-done.1
  8.9 14.5 %standardize.1.s_ref = bf16[8,3600,128]{2,1,0:T(8,128)(2,1)} custom-call(bf16[3600,8,128]{2,1,0:T(8,128)(2,1)} %x_hbm.1, s32[8,128]{1,0:T(8,128)S(1)} %copy-done, bf16[3,240,256]{2,1,0:T(8,128)(2,1)S(1)} %copy-done.1), custom_call_target="tpu_custom_call" | custom-call | flops 6000000000 | bytes 15000000 | tf_op jit(solution)/shard_map/standardize/pallas_call | solution.py:110
  23.5 5.2 %edges.1 = bf16[16,3600]{1,0:T(8,128)(2,1)S(1)} custom-call(bf16[8,3600,128]{2,1,0:T(8,128)(2,1)} %standardize.1.s_ref), custom_call_target="tpu_custom_call" | custom-call | tf_op jit(solution)/shard_map/edges/pallas_call | solution.py:156
  28.6 4.1 %collective-permute-start.2 = (bf16[16,3600]{1,0:T(8,128)(2,1)S(1)}, bf16[16,3600]{1,0:T(8,128)(2,1)S(1)}, u32[]{:S(2)}, u32[]{:S(2)}) collective-permute-start(bf16[16,3600]{1,0:T(8,128)(2,1)S(1)} %edges.1), channel_id=1, source_target_pairs={{0,1},{1,2},{2,3},{4,5},{5,6},{6,7},{8,9},{9,10},{10,11},{12,13},{... | collective-permute-start | bytes 345608 | tf_op jit(solution)/shard_map/ppermute | solution.py:361
  32.7 1.3 %collective-permute-start.3 = (bf16[16,3600]{1,0:T(8,128)(2,1)S(1)}, bf16[16,3600]{1,0:T(8,128)(2,1)S(1)}, u32[]{:S(2)}, u32[]{:S(2)}) collective-permute-start(bf16[16,3600]{1,0:T(8,128)(2,1)S(1)} %edges.1), channel_id=1, source_target_pairs={{1,0},{2,1},{3,2},{5,4},{6,5},{7,6},{9,8},{10,9},{11,10},{13,12},{... | collective-permute-start | bytes 345608 | tf_op jit(solution)/shard_map/ppermute | solution.py:366
  34.0 2.5 %slice_bitcast_fusion = (bf16[3600,128]{1,0:T(8,128)(2,1)S(1)}, bf16[3600,128]{1,0:T(8,128)(2,1)}) fusion(bf16[8,3600,128]{2,1,0:T(8,128)(2,1)} %standardize.1.s_ref), kind=kLoop, calls=%fused_computation | loop fusion | bytes 3686400 | tf_op jit(solution)/shard_map/squeeze | solution.py:392
  36.5 3.9 %collective-permute-start = (bf16[3600,128]{1,0:T(8,128)(2,1)}, bf16[3600,128]{1,0:T(8,128)(2,1)S(1)}, u32[]{:S(2)}, u32[]{:S(2)}) collective-permute-start(bf16[3600,128]{1,0:T(8,128)(2,1)} %get-tuple-element.10), channel_id=1, source_target_pairs={{0,4},{4,8},{8,12},{12,16},{16,20},{20,24},{24,28},{1,5},{5,9},{9,... | collective-permute-start | bytes 2764808 | tf_op jit(solution)/shard_map/ppermute | solution.py:361
  40.5 1.9 %collective-permute-start.1 = (bf16[3600,128]{1,0:T(8,128)(2,1)S(1)}, bf16[3600,128]{1,0:T(8,128)(2,1)S(1)}, u32[]{:S(2)}, u32[]{:S(2)}) collective-permute-start(bf16[3600,128]{1,0:T(8,128)(2,1)S(1)} %get-tuple-element.9), channel_id=1, source_target_pairs={{4,0},{8,4},{12,8},{16,12},{20,16},{24,20},{28,24},{5,1},{9,5},{13... | collective-permute-start | bytes 2764808 | tf_op jit(solution)/shard_map/ppermute | solution.py:366
  42.5 0.1 constant_dynamic-update-slice_fusion.7
  42.6 0.1 constant_dynamic-update-slice_fusion.6
  42.6 0.1 constant_dynamic-update-slice_fusion.5
  42.7 0.1 constant_dynamic-update-slice_fusion.4
  42.8 0.1 constant_dynamic-update-slice_fusion.3
  42.9 0.1 constant_dynamic-update-slice_fusion.2
  43.0 0.1 constant_dynamic-update-slice_fusion.1
  43.0 0.1 constant_dynamic-update-slice_fusion
  43.2 1.9 %collective-permute-start.5 = (bf16[16,3600]{1,0:T(8,128)(2,1)S(1)}, bf16[16,3600]{1,0:T(8,128)(2,1)S(1)}, u32[]{:S(2)}, u32[]{:S(2)}) collective-permute-start(bf16[16,3600]{1,0:T(8,128)(2,1)S(1)} %pad_maximum_fusion), channel_id=1, source_target_pairs={{4,0},{8,4},{12,8},{16,12},{20,16},{24,20},{28,24},{5,1},{9,5},{13... | collective-permute-start | bytes 345608 | tf_op jit(solution)/shard_map/ppermute | solution.py:366
  45.1 3.8 %collective-permute-start.4 = (bf16[16,3600]{1,0:T(8,128)(2,1)S(1)}, bf16[16,3600]{1,0:T(8,128)(2,1)S(1)}, u32[]{:S(2)}, u32[]{:S(2)}) collective-permute-start(bf16[16,3600]{1,0:T(8,128)(2,1)S(1)} %pad_maximum_fusion), channel_id=1, source_target_pairs={{0,4},{4,8},{8,12},{12,16},{16,20},{20,24},{24,28},{1,5},{5,9},{9,... | collective-permute-start | bytes 345608 | tf_op jit(solution)/shard_map/ppermute | solution.py:361
  49.0 28.9 %collective-permute-done.5 = bf16[16,3600]{1,0:T(8,128)(2,1)S(1)} collective-permute-done((bf16[16,3600]{1,0:T(8,128)(2,1)S(1)}, bf16[16,3600]{1,0:T(8,128)(2,1)S(1)}, u32[]{:S(2)}, u32[]{:S(2)}) %collective-permute-start.5) | collective-permute-done | bytes 115232 | tf_op jit(solution)/shard_map/ppermute | solution.py:366
  78.0 0.6 concatenate.7.side_ref
  78.6 17.6 %average.1 = (bf16[8,3600,128]{2,1,0:T(8,128)(2,1)}, f32[8,128]{1,0:T(8,128)S(1)}) custom-call(bf16[8,3600,128]{2,1,0:T(8,128)(2,1)} %standardize.1.s_ref, bf16[3600,128]{1,0:T(8,128)(2,1)S(1)} %collective-permute-done.top_ref, bf16[3600,128]{1,0:T(8,128)(2,1)S(1)} %collective-permute-done.1.bottom_ref, bf16[32,3600]{1,0:T(8,128)(2,1)S(1)} %concatenate.7.side_ref, ...), custom_call_target="tpu_custom_call" | custom-call | flops 12000000000 | bytes 17000000 | tf_op jit(solution)/shard_map/average/pallas_call | solution.py:268
  96.2 14.5 %score.1 = f32[2,4,8,128]{3,2,1,0:T(8,128)} custom-call(bf16[2,512,3600]{2,1,0:T(8,128)(2,1)} %all-gather.2.cloned.1.call-done.d_ref, bf16[8,3600,128]{2,1,0:T(8,128)(2,1)} %get-tuple-element.7.a_ref, f32[8,128]{1,0:T(8,128)S(1)} %get-tuple-element.8.inv_ref), custom_call_target="tpu_custom_call" | custom-call | flops 7500000256 | bytes 15000000 | tf_op jit(solution)/shard_map/score/pallas_call | solution.py:340
  (22 shorter events, 0.2 us)
Async XLA Ops:
  6.5 89.7 %all-gather.2.cloned.1.call-start = ((), (), s32[]{:S(2)}) async-start(), calls=%async_computation | async-start | bytes 7839744 | tf_op jit(solution)/shard_map/all_gather | solution.py:388
  7.3 0.7 copy-start
  7.9 1.0 copy-start.1
  23.4 21.7 %copy-start.2 = (s32[8,8,128]{2,1,0:T(8,128)S(1)}, s32[8,8,128]{2,1,0:T(8,128)}, u32[]{:S(2)}) copy-start(s32[8,8,128]{2,1,0:T(8,128)} %param.7) | copy-start | bytes 98308
  28.6 14.5 %collective-permute-start.2 = (bf16[16,3600]{1,0:T(8,128)(2,1)S(1)}, bf16[16,3600]{1,0:T(8,128)(2,1)S(1)}, u32[]{:S(2)}, u32[]{:S(2)}) collective-permute-start(bf16[16,3600]{1,0:T(8,128)(2,1)S(1)} %edges.1), channel_id=1, source_target_pairs={{0,1},{1,2},{2,3},{4,5},{5,6},{6,7},{8,9},{9,10},{10,11},{12,13},{... | collective-permute-start | bytes 345608 | tf_op jit(solution)/shard_map/ppermute | solution.py:361
  32.7 10.4 %collective-permute-start.3 = (bf16[16,3600]{1,0:T(8,128)(2,1)S(1)}, bf16[16,3600]{1,0:T(8,128)(2,1)S(1)}, u32[]{:S(2)}, u32[]{:S(2)}) collective-permute-start(bf16[16,3600]{1,0:T(8,128)(2,1)S(1)} %edges.1), channel_id=1, source_target_pairs={{1,0},{2,1},{3,2},{5,4},{6,5},{7,6},{9,8},{10,9},{11,10},{13,12},{... | collective-permute-start | bytes 345608 | tf_op jit(solution)/shard_map/ppermute | solution.py:366
  36.5 42.0 %collective-permute-start = (bf16[3600,128]{1,0:T(8,128)(2,1)}, bf16[3600,128]{1,0:T(8,128)(2,1)S(1)}, u32[]{:S(2)}, u32[]{:S(2)}) collective-permute-start(bf16[3600,128]{1,0:T(8,128)(2,1)} %get-tuple-element.10), channel_id=1, source_target_pairs={{0,4},{4,8},{8,12},{12,16},{16,20},{20,24},{24,28},{1,5},{5,9},{9,... | collective-permute-start | bytes 2764808 | tf_op jit(solution)/shard_map/ppermute | solution.py:361
  40.5 38.1 %collective-permute-start.1 = (bf16[3600,128]{1,0:T(8,128)(2,1)S(1)}, bf16[3600,128]{1,0:T(8,128)(2,1)S(1)}, u32[]{:S(2)}, u32[]{:S(2)}) collective-permute-start(bf16[3600,128]{1,0:T(8,128)(2,1)S(1)} %get-tuple-element.9), channel_id=1, source_target_pairs={{4,0},{8,4},{12,8},{16,12},{20,16},{24,20},{28,24},{5,1},{9,5},{13... | collective-permute-start | bytes 2764808 | tf_op jit(solution)/shard_map/ppermute | solution.py:366
  43.2 34.7 %collective-permute-start.5 = (bf16[16,3600]{1,0:T(8,128)(2,1)S(1)}, bf16[16,3600]{1,0:T(8,128)(2,1)S(1)}, u32[]{:S(2)}, u32[]{:S(2)}) collective-permute-start(bf16[16,3600]{1,0:T(8,128)(2,1)S(1)} %pad_maximum_fusion), channel_id=1, source_target_pairs={{4,0},{8,4},{12,8},{16,12},{20,16},{24,20},{28,24},{5,1},{9,5},{13... | collective-permute-start | bytes 345608 | tf_op jit(solution)/shard_map/ppermute | solution.py:366
  45.1 32.8 %collective-permute-start.4 = (bf16[16,3600]{1,0:T(8,128)(2,1)S(1)}, bf16[16,3600]{1,0:T(8,128)(2,1)S(1)}, u32[]{:S(2)}, u32[]{:S(2)}) collective-permute-start(bf16[16,3600]{1,0:T(8,128)(2,1)S(1)} %pad_maximum_fusion), channel_id=1, source_target_pairs={{0,4},{4,8},{8,12},{12,16},{16,20},{20,24},{24,28},{1,5},{5,9},{9,... | collective-permute-start | bytes 345608 | tf_op jit(solution)/shard_map/ppermute | solution.py:361
Sparse Core Ops, SparseCore 0:
  10.3 85.6 all-gather.1
where the time goes:
time: 118 us
  Pallas kernels  51.8 us (44%)
  waiting for transfers between devices  29.6 us (25%)
  starting transfers between devices  16.9 us (14%)
  between operations  13.6 us (12%)
  local copies, waits for them, and re-layouts  4.86 us (4%)
    ppermute x3, waiting for transfers between devices, from_high(): return lax.ppermute(x, axis, [(i + 1, i) for i in range(count - 1)])  28.9 us
    pallas_call x1, Pallas kernels, average(): pl.pallas_call(average_kernel, out_shape=(jax.ShapeDtypeStruct((rows, pix...  17.6 us
    pallas_call x1, Pallas kernels, standardize(): pl.pallas_call(standardize_kernel, grid=(rows // 2,), in_specs=[pl.BlockS...  14.5 us
    pallas_call x1, Pallas kernels, score(): pl.pallas_call(score_kernel, grid=(panels, entries // size), in_specs=[pl...  14.5 us
    ppermute x3, starting transfers between devices, from_low(): return lax.ppermute(x, axis, [(i, i + 1) for i in range(count - 1)])  11.8 us
    pallas_call x1, Pallas kernels, edges(): pl.pallas_call(edges_kernel, out_shape=jax.ShapeDtypeStruct((2 * rows, pi...  5.18 us
    ppermute x3, starting transfers between devices, from_high(): return lax.ppermute(x, axis, [(i + 1, i) for i in range(count - 1)])  5.13 us
    squeeze x1, local copies, waits for them, and re-layouts, on_device(): bottom = from_high(standard[0], 'strip')  2.54 us
  transfers between devices with their start and end apart: 7, of which 1 were waited for; matrix products, arithmetic and copies ran while one was open for 3% of the time, Pallas kernels for 32%

commit v1 on v0

v1 whole, which is shorter than its diff:
```python
import functools

import jax
import jax.numpy as jnp
import ml_dtypes
import numpy as np
from jax import lax
from jax.experimental import pallas as pl
from jax.experimental.pallas import tpu as pltpu
from jax.sharding import PartitionSpec as P

PH = 60
TOP = 4
QUAD = 4
GROUPS = PH // QUAD
TILE = QUAD * QUAD
CHUNK = GROUPS * TILE
DEPTH = 256
LANES = 128
SIDES = 32

epsilon = 1e-05
nlpar_scale = 2.0
MIB = 1 << 20


def blur_matrix():
    at = np.arange(PH, dtype=np.float32)
    spread_px = np.float32(PH / 8.0)
    gap = at[:, None] - at[None, :]
    profile = np.exp(-(gap * gap) / (np.float32(2.0) * spread_px * spread_px))
    profile = profile / profile.sum(axis=1, keepdims=True)
    return profile.astype(ml_dtypes.bfloat16).astype(np.float32)


def pass_matrices():
    kernel = blur_matrix()
    index = np.arange(CHUNK)
    quad, row, col = index // TILE, (index // QUAD) % QUAD, index % QUAD
    along = quad * QUAD + col
    columns = kernel[along[:, None], along[None, :]] * (row[:, None] == row[None, :])
    down = quad * QUAD + row
    rows = kernel[down[:, None], down[None, :]] * (col[:, None] == col[None, :])
    natural = row * PH + along
    order = (index[:, None] == natural[None, :]).astype(np.float32)
    out = np.zeros((3, CHUNK, DEPTH), np.float32)
    out[0, :, :CHUNK], out[1, :, :CHUNK], out[2, :, :CHUNK] = columns, rows, order
    return out.astype(ml_dtypes.bfloat16)


def tiles_of(pieces):
    return jnp.concatenate(pieces + [pieces[-1]], axis=0)


def on_chip(x):
    return pltpu.with_memory_space_constraint(x, pltpu.VMEM)


def in_hbm(x):
    return pltpu.with_memory_space_constraint(x, pltpu.HBM)


WHOLE = pl.BlockSpec(memory_space=pltpu.VMEM)
APART = pl.BlockSpec(memory_space=pl.ANY)
SHORT = pl.CostEstimate(flops=1000, bytes_accessed=1000, transcendentals=0)
TOKEN = jax.ShapeDtypeStruct((8, LANES), jnp.float32)


def mark(ref):
    ref[...] = jnp.zeros(ref.shape, ref.dtype)


def standard_rows(both, mat_ref, half, corr, sq, stores):
    for g in range(GROUPS):
        rhs = tiles_of([both(quad, slice(g * TILE, (g + 1) * TILE)) for quad in range(GROUPS)])
        out = jnp.dot(mat_ref[0], rhs, preferred_element_type=jnp.float32)
        half[g] = out.astype(jnp.bfloat16)

    total = jnp.zeros((8, 2 * LANES), jnp.float32)
    squares = jnp.zeros((8, 2 * LANES), jnp.float32)
    for quad in range(GROUPS):
        rhs = tiles_of([half[g, pl.ds(quad * TILE, TILE), :] for g in range(GROUPS)])
        background = jnp.dot(mat_ref[1], rhs, preferred_element_type=jnp.float32)
        corrected = both(quad, slice(None)).astype(jnp.float32) - background
        corr[quad] = corrected
        folded = corrected.reshape(CHUNK // 8, 8, 2 * LANES)
        total = total + jnp.sum(folded, axis=0)
        squares = squares + jnp.sum(folded * folded, axis=0)
    pixels = GROUPS * CHUNK
    mean = jnp.sum(total, axis=0, keepdims=True) / pixels
    variance = jnp.sum(squares, axis=0, keepdims=True) / pixels - mean * mean
    scale = 1.0 / jnp.sqrt(jnp.maximum(variance, 0.0) + epsilon)
    for quad in range(GROUPS):
        sq[quad] = ((corr[quad] - mean) * scale).astype(jnp.bfloat16)
    for g in range(GROUPS):
        rhs = tiles_of([sq[quad, pl.ds(g * TILE, TILE), :] for quad in range(GROUPS)])
        out = jnp.dot(mat_ref[2], rhs, preferred_element_type=jnp.float32).astype(jnp.bfloat16)
        for side, store in enumerate(stores):
            store(slice(g * CHUNK, (g + 1) * CHUNK), out[:, side * LANES : (side + 1) * LANES])


def border_kernel(x_hbm, mask_hbm, mat_hbm, xq_hbm, first, last, token, mask_ref, mat_ref, xq, ends, raw, half, corr, sq, sems):
    rows = raw.shape[2]
    mark(token)

    def fetch(g):
        return pltpu.make_async_copy(x_hbm.at[pl.ds(g * CHUNK, CHUNK)], raw.at[g], sems.at[g])

    mask_copy = pltpu.make_async_copy(mask_hbm, mask_ref, sems.at[GROUPS])
    matrices = pltpu.make_async_copy(mat_hbm, mat_ref, sems.at[GROUPS + 1])
    keep = pltpu.make_async_copy(xq, xq_hbm, sems.at[GROUPS + 2])
    mask_copy.start()
    for g in range(GROUPS):
        fetch(g).start()
    matrices.start()
    mask_copy.wait()
    mask = mask_ref[...].astype(jnp.bfloat16)[None]
    for g in range(GROUPS):
        fetch(g).wait()
        for quad in range(GROUPS):
            piece = jnp.concatenate(
                [raw[g, pl.ds(row * PH + quad * QUAD, QUAD)] for row in range(QUAD)], axis=0
            )
            tile = jnp.swapaxes(piece * mask, 0, 1)
            span = slice(g * TILE, (g + 1) * TILE)
            xq[:, quad, span, :] = tile[1 : rows - 1]
            ends[0, quad, span, :] = tile[0]
            ends[1, quad, span, :] = tile[rows - 1]
    keep.start()
    matrices.wait()

    def both(quad, span):
        return jnp.concatenate([ends[0, quad, span, :], ends[1, quad, span, :]], axis=1)

    def store(ref):
        def put(span, value):
            ref[span, :] = value

        return put

    standard_rows(both, mat_ref, half, corr, sq, [store(first), store(last)])
    keep.wait()


def row_scratch(cols):
    return [
        pltpu.VMEM((GROUPS, CHUNK, 2 * cols), jnp.bfloat16),
        pltpu.VMEM((GROUPS, CHUNK, 2 * cols), jnp.float32),
        pltpu.VMEM((GROUPS, CHUNK, 2 * cols), jnp.bfloat16),
    ]


def border(patterns, scan_mask, matrices):
    pixels, rows, cols = patterns.shape
    bf16 = jnp.bfloat16
    return pl.pallas_call(
        border_kernel,
        in_specs=[APART] * 3,
        out_specs=(APART, WHOLE, WHOLE, WHOLE),
        out_shape=(
            pltpu.HBM((rows - 2, GROUPS, CHUNK, cols), bf16),
            pltpu.VMEM((pixels, cols), bf16),
            pltpu.VMEM((pixels, cols), bf16),
            TOKEN,
        ),
        scratch_shapes=[
            pltpu.VMEM((rows, cols), scan_mask.dtype),
            pltpu.VMEM(matrices.shape, bf16),
            pltpu.VMEM((rows - 2, GROUPS, CHUNK, cols), bf16),
            pltpu.VMEM((2, GROUPS, CHUNK, cols), bf16),
            pltpu.VMEM((GROUPS, CHUNK, rows, cols), bf16),
        ]
        + row_scratch(cols)
        + [pltpu.SemaphoreType.DMA((GROUPS + 3,))],
        compiler_params=pltpu.CompilerParams(vmem_limit_bytes=26 * MIB),
        cost_estimate=SHORT,
        name="border",
    )(in_hbm(patterns), in_hbm(scan_mask), in_hbm(matrices))


def interior_kernel(xq_hbm, mat_hbm, _, s_ref, token, mat_ref, xq, half, corr, sq, sems):
    mark(token)
    pairs = s_ref.shape[0] // 2
    matrices = pltpu.make_async_copy(mat_hbm, mat_ref, sems.at[2])

    def fetch(i, slot):
        return pltpu.make_async_copy(xq_hbm.at[pl.ds(2 * i, 2)], xq.at[slot], sems.at[slot])

    fetch(0, 0).start()
    matrices.start()
    matrices.wait()

    def pair(i, carry):
        slot = lax.rem(i, 2)
        fetch(i, slot).wait()

        @pl.when(i + 1 < pairs)
        def _():
            fetch(i + 1, 1 - slot).start()

        def both(quad, span):
            return jnp.concatenate([xq[slot, 0, quad, span, :], xq[slot, 1, quad, span, :]], axis=1)

        def store(side):
            def put(span, value):
                s_ref[2 * i + side, span, :] = value

            return put

        standard_rows(both, mat_ref, half, corr, sq, [store(0), store(1)])
        return carry

    lax.fori_loop(0, pairs, pair, 0)


def interior(xq, matrices, earlier):
    rows, _, _, cols = xq.shape
    pixels = GROUPS * CHUNK
    return pl.pallas_call(
        interior_kernel,
        in_specs=[APART, APART, WHOLE],
        out_specs=(WHOLE, WHOLE),
        out_shape=(pltpu.VMEM((rows, pixels, cols), jnp.bfloat16), TOKEN),
        scratch_shapes=[
            pltpu.VMEM(matrices.shape, jnp.bfloat16),
            pltpu.VMEM((2, 2, GROUPS, CHUNK, cols), jnp.bfloat16),
        ]
        + row_scratch(cols)
        + [pltpu.SemaphoreType.DMA((3,))],
        compiler_params=pltpu.CompilerParams(vmem_limit_bytes=16 * MIB),
        cost_estimate=SHORT,
        name="interior",
    )(in_hbm(xq), in_hbm(matrices), earlier)


def row_of(refs, rows):
    above, first, middle, last, below = refs

    def row(r):
        if 1 <= r < rows - 1:
            return middle.at[r - 1]
        return {-1: above, 0: first, rows - 1: last, rows: below}[r]

    return row


def diagonals(product, at_sub, at_lane):
    return [
        jnp.sum(jnp.where(at_sub == at_lane + d, product, 0.0), axis=0, keepdims=True)
        for d in (-1, 0, 1)
    ]


PER_ROW = 8


def products_kernel(*refs):
    left, right, out = refs[-3:]
    rows = refs[2].shape[0] + 2
    row = row_of(refs[:5], rows)
    cols = refs[0].shape[1]
    f32 = jnp.float32
    at_sub = lax.broadcasted_iota(jnp.int32, (cols, cols), 0)
    at_lane = lax.broadcasted_iota(jnp.int32, (cols, cols), 1)
    firsts, lasts = [], []
    for r in range(-1, rows + 1):
        here = row(r)[...]
        across = here.T
        firsts.append(across[:1])
        lasts.append(across[cols - 1 :])
        pieces = [here]
        if r < rows:
            pieces.append(row(r + 1)[...])
        product = jnp.dot(across, jnp.concatenate(pieces, axis=1), preferred_element_type=f32)
        own = diagonals(product[:, :cols], at_sub, at_lane)
        vectors = [own[1], own[0]]
        if r < rows:
            vectors += diagonals(product[:, cols:], at_sub, at_lane)
        vectors += [jnp.zeros((1, cols), f32)] * (PER_ROW - len(vectors))
        out[r + 1] = jnp.concatenate(vectors, axis=0)
    blank = [jnp.zeros((SIDES // 2 - len(firsts), here.shape[0]), firsts[0].dtype)]
    left[...] = jnp.concatenate(firsts + blank, axis=0)
    right[...] = jnp.concatenate(lasts + blank, axis=0)


def products(block, *earlier):
    rows = block[2].shape[0] + 2
    pixels, cols = block[0].shape
    one = jax.ShapeDtypeStruct((SIDES // 2, pixels), jnp.bfloat16)
    return pl.pallas_call(
        products_kernel,
        in_specs=[WHOLE] * (5 + len(earlier)),
        out_specs=(WHOLE,) * 3,
        out_shape=(one, one, jax.ShapeDtypeStruct((rows + 2, PER_ROW, cols), jnp.float32)),
        compiler_params=pltpu.CompilerParams(vmem_limit_bytes=12 * MIB),
        cost_estimate=SHORT,
        name="products",
    )(*map(on_chip, block), *earlier)


def average_kernel(*refs):
    left_ref, right_ref, dot_ref, usable_ref = refs[5:9]
    a_ref, inv_ref, sides, weights = refs[-4:]
    rows, pixels, cols = a_ref.shape
    row = row_of(refs[:5], rows)
    f32 = jnp.float32
    at_sub = lax.broadcasted_iota(jnp.int32, (cols, cols), 0)
    at_lane = lax.broadcasted_iota(jnp.int32, (cols, cols), 1)
    lane = lax.broadcasted_iota(jnp.int32, (1, cols), 1)

    side = jnp.concatenate([left_ref[...], right_ref[...]], axis=0)
    side32 = side.astype(f32)
    side_norm = jnp.sum(side32 * side32, axis=1, keepdims=True)
    pad = jnp.concatenate([side32, jnp.zeros((cols - SIDES, pixels), f32)], axis=0)
    for start in range(0, pixels, LANES):
        width = min(LANES, pixels - start)
        sides[pl.ds(start, width), :] = pad[:, start : start + width].T.astype(jnp.bfloat16)

    def shifted(vector, dc):
        if dc == 0:
            return vector
        return pltpu.roll(vector, (-dc) % cols, 1)

    def kept(r, k):
        return dot_ref[r + 1, pl.ds(k, 1), :]

    for r in range(rows):
        to_side = jnp.dot(side, row(r)[...], preferred_element_type=f32)
        weight = {}
        slot = 0
        total = jnp.ones((1, cols), f32)
        for dr in (-1, 0, 1):
            for dc in (-1, 0, 1):
                if dr == 0 and dc == 0:
                    continue
                if dr == -1:
                    dot = kept(r - 1, 3 + dc)
                elif dr == 1:
                    dot = shifted(kept(r, 3 - dc), dc)
                else:
                    dot = kept(r, 1) if dc == -1 else shifted(kept(r, 1), 1)
                other = shifted(kept(r + dr, 0), dc)
                if dc != 0:
                    k = r + dr + 1 + (0 if dc < 0 else 16)
                    end = 0 if dc < 0 else cols - 1
                    dot = jnp.where(lane == end, to_side[k : k + 1, :], dot)
                    other = jnp.where(lane == end, side_norm[k : k + 1, :], other)
                distance = jnp.maximum(kept(r, 0) + other - 2.0 * dot, 0.0) / pixels
                weight[dr, dc] = usable_ref[slot, pl.ds(r, 1), :] * jnp.exp(-distance / nlpar_scale)
                total = total + weight[dr, dc]
                slot += 1
        for dr in (-1, 0, 1):
            block = jnp.zeros((cols, cols), f32)
            for dc in (-1, 0, 1):
                w = jnp.ones((1, cols), f32) if dr == 0 and dc == 0 else weight[dr, dc]
                block = jnp.where(at_sub == at_lane + dc, w, block)
            weights[dr + 1] = block
        block = jnp.zeros((cols, cols), f32)
        for dr in (-1, 0, 1):
            for dc in (-1, 1):
                k = r + dr + 1 + (0 if dc < 0 else 16)
                end = 0 if dc < 0 else cols - 1
                block = jnp.where((at_sub == k) & (at_lane == end), weight[dr, dc], block)
        weights[3] = block

        full = weights[...].reshape(4 * cols, cols)
        high = full.astype(jnp.bfloat16)
        low = (full - high.astype(f32)).astype(jnp.bfloat16)
        split = jnp.concatenate([high, low], axis=1)
        inverse = 1.0 / total
        squares = jnp.zeros((8, cols), f32)
        for g in range(GROUPS):
            span = slice(g * CHUNK, (g + 1) * CHUNK)
            lhs = jnp.concatenate(
                [row(r - 1)[span, :], row(r)[span, :], row(r + 1)[span, :], sides[span, :]], axis=1
            )
            out = jnp.dot(lhs, split, preferred_element_type=f32)
            mean = ((out[:, :cols] + out[:, cols:]) * inverse).astype(jnp.bfloat16)
            a_ref[r, span, :] = mean
            mean32 = mean.astype(f32).reshape(CHUNK // 8, 8, cols)
            squares = squares + jnp.sum(mean32 * mean32, axis=0)
        energy = jnp.sum(squares, axis=0, keepdims=True) / pixels
        inv_ref[pl.ds(r, 1), :] = 1.0 / jnp.sqrt(energy + epsilon)


def average(block, left, right, dots, usable, *earlier):
    rows = block[2].shape[0] + 2
    pixels, cols = block[0].shape
    return pl.pallas_call(
        average_kernel,
        in_specs=[WHOLE] * (9 + len(earlier)),
        out_specs=(WHOLE, WHOLE),
        out_shape=(
            pltpu.VMEM((rows, pixels, cols), jnp.bfloat16),
            jax.ShapeDtypeStruct((rows, cols), jnp.float32),
        ),
        scratch_shapes=[
            pltpu.VMEM((pixels, cols), jnp.bfloat16),
            pltpu.VMEM((4, cols, cols), jnp.float32),
        ],
        compiler_params=pltpu.CompilerParams(vmem_limit_bytes=8 * MIB),
        cost_estimate=SHORT,
        name="average",
    )(*map(on_chip, block), left, right, dots, usable, *earlier)


def insert(best, new):
    kept = []
    for slot, held in enumerate(best):
        kept.append(jnp.maximum(held, new))
        if slot < len(best) - 1:
            new = jnp.minimum(held, new)
    return kept


def merge_sublanes(best):
    for shift in (4, 2, 1):
        other = [pltpu.roll(b, shift, 0) for b in best]
        m = [jnp.maximum(best[i], other[3 - i]) for i in range(4)]
        a, c = jnp.maximum(m[0], m[2]), jnp.minimum(m[0], m[2])
        b, d = jnp.maximum(m[1], m[3]), jnp.minimum(m[1], m[3])
        best = [jnp.maximum(a, b), jnp.minimum(a, b), jnp.maximum(c, d), jnp.minimum(c, d)]
    return best


def score_kernel(count, a_ref, best_ref, *refs):
    pieces, last = refs[:count], refs[count:]
    out = last[-1]
    rows, pixels, cols = a_ref.shape
    f32 = jnp.float32
    panels = pieces[0].shape[0]
    entries = jnp.concatenate([piece[k] for k in range(panels) for piece in pieces], axis=0)
    each = sum(piece.shape[1] for piece in pieces)
    entries32 = entries.astype(f32)
    energy = jnp.sum(entries32 * entries32, axis=1, keepdims=True) / pixels
    inv_entry = 1.0 / jnp.sqrt(energy + epsilon) / pixels
    for r in range(0, rows, 2):
        block = jnp.concatenate([a_ref[r], a_ref[r + 1]], axis=1)
        scores = jnp.dot(entries, block, preferred_element_type=f32) * inv_entry
        for k in range(panels):
            for half in range(2):
                held = [best_ref[k, j, r + half] for j in range(TOP)]
                for e in range(k * each, (k + 1) * each, 8):
                    held = insert(held, scores[e : e + 8, half * cols : (half + 1) * cols])
                if len(last) > 1:
                    inv = last[0][pl.ds(r + half, 1), :]
                    held = merge_sublanes(held)
                    for j in range(TOP):
                        out[k, j, pl.ds(r + half, 1), :] = held[j][:1] * inv
                else:
                    for j in range(TOP):
                        out[k, j, r + half] = held[j]


def score(averaged, best, pieces, inv_pattern=None):
    last = [] if inv_pattern is None else [inv_pattern]
    panels, top, rows, sublanes, cols = best.shape
    shape = (panels, top, rows, cols) if last else best.shape
    out = jax.ShapeDtypeStruct(shape, jnp.float32)
    return pl.pallas_call(
        functools.partial(score_kernel, len(pieces)),
        in_specs=[WHOLE] * (2 + len(pieces) + len(last)),
        out_specs=WHOLE,
        out_shape=out,
        compiler_params=pltpu.CompilerParams(vmem_limit_bytes=14 * MIB),
        cost_estimate=SHORT,
        name="score",
    )(on_chip(averaged), best, *pieces, *last)


def exchange(x, axis, masks):
    count = lax.axis_size(axis)
    return lax.ppermute(x, axis, [(i, i ^ masks[i & 1]) for i in range(count)])


def power_of_two(n):
    return n & (n - 1) == 0


def hold(x, *earlier):
    def nothing(*refs):
        pass

    return pl.pallas_call(
        nothing,
        in_specs=[APART] + [WHOLE] * len(earlier),
        out_specs=APART,
        out_shape=jax.ShapeDtypeStruct(x.shape, x.dtype),
        input_output_aliases={0: 0},
        compiler_params=pltpu.CompilerParams(vmem_limit_bytes=MIB),
        cost_estimate=SHORT,
        name="hold",
    )(x, *earlier)


def join_kernel(count, *refs):
    parts, (out, token, sems) = refs[:count], refs[-3:]
    mark(token)
    copies, at = [], 0
    for i, part in enumerate(parts):
        size = part.shape[1]
        copies.append(pltpu.make_async_copy(part, out.at[:, pl.ds(at, size)], sems.at[i]))
        at += size
    for copy in copies:
        copy.start()
    for copy in copies:
        copy.wait()


def join(parts, *earlier):
    panels, _, pixels = parts[0].shape
    if any(part.shape[1] % 16 for part in parts):
        whole = jnp.concatenate(parts, axis=1)
        return hold(whole, *earlier), jnp.zeros(TOKEN.shape, TOKEN.dtype)
    size = sum(part.shape[1] for part in parts)
    return pl.pallas_call(
        functools.partial(join_kernel, len(parts)),
        in_specs=[APART] * len(parts) + [WHOLE] * len(earlier),
        out_specs=(APART, WHOLE),
        out_shape=(jax.ShapeDtypeStruct((panels, size, pixels), parts[0].dtype), TOKEN),
        scratch_shapes=[pltpu.SemaphoreType.DMA((len(parts),))],
        compiler_params=pltpu.CompilerParams(vmem_limit_bytes=MIB),
        cost_estimate=SHORT,
        name="join",
    )(*parts, *earlier)


def gathers(strip, line):
    return power_of_two(strip) and power_of_two(line) and strip > 2 and line > 1


def strip_masks(strip):
    bits = [1 << i for i in range(1, strip.bit_length() - 1)]
    return list(zip(bits, reversed(bits)))


def from_low(x, axis):
    count = lax.axis_size(axis)
    return lax.ppermute(x, axis, [(i, i + 1) for i in range(count - 1)])


def from_high(x, axis):
    count = lax.axis_size(axis)
    return lax.ppermute(x, axis, [(i + 1, i) for i in range(count - 1)])


def usable_neighbours(neighbour_mask):
    _, rows, cols = neighbour_mask.shape
    row_at = lax.axis_index("strip") * rows + jnp.arange(rows, dtype=jnp.int32)
    col_at = lax.axis_index("dict") * cols + jnp.arange(cols, dtype=jnp.int32)
    all_rows = rows * lax.axis_size("strip")
    all_cols = cols * lax.axis_size("dict")
    inside = []
    for dr in (-1, 0, 1):
        for dc in (-1, 0, 1):
            if dr == 0 and dc == 0:
                continue
            row_ok = (row_at + dr >= 0) & (row_at + dr < all_rows)
            col_ok = (col_at + dc >= 0) & (col_at + dc < all_cols)
            inside.append(row_ok[:, None] & col_ok[None, :])
    return (jnp.stack(inside) & (neighbour_mask == 1)).astype(jnp.float32)


def on_device(patterns, scan_mask, neighbour_mask, dictionary):
    rows, cols = scan_mask.shape
    strip, line = lax.axis_size("strip"), lax.axis_size("dict")
    alone = not gathers(strip, line)
    matrices = jnp.asarray(pass_matrices())
    usable = usable_neighbours(neighbour_mask)
    best = jnp.full((dictionary.shape[0], TOP, rows, 8, cols), -jnp.inf, jnp.float32)
    if not alone:
        ways = strip_masks(strip)
        near = dictionary
        near_new = exchange(near, "strip", ways[0])
        far = [exchange(dictionary, "dict", (mask, mask)) for mask in range(1, line)]

    xq, first, last, bordered = border(patterns, scan_mask, matrices)
    above = from_low(last, "strip")
    below = from_high(first, "strip")
    done = bordered
    if not alone:
        for way in ways[1:]:
            near, done = join([near, near_new], bordered)
            near_new = exchange(near, "strip", way)

    middle, filled = interior(xq, matrices, done)
    block = (above, first, middle, last, below)
    joined = [filled]
    if not alone:
        near, done = join([near, near_new], filled)
        near_other = exchange(near, "strip", (1, 1))
        far, done = join(far, done)
        far_new = exchange(far, "strip", ways[0])
        joined = [done]

    own_left, own_right, dots = products(block, *joined)
    left = from_low(own_right, "dict")
    right = from_high(own_left, "dict")
    joined = []
    if not alone:
        for way in ways[1:]:
            far, done = join([far, far_new], dots)
            far_new = exchange(far, "strip", way)
        joined = [done]
        far_other = exchange(far, "strip", (1, 1))

    averaged, inv_pattern = average(block, left, right, dots, usable, *joined)
    if alone:
        whole = lax.all_gather(dictionary, ("strip", "dict"), axis=1, tiled=True)
        return score(averaged, best, [whole], inv_pattern)
    best = score(averaged, best, [near, near_other])
    far_new = hold(far_new, best)
    far_new_other = exchange(far_new, "strip", (1, 1))
    best = score(averaged, best, [far, far_other])
    best = score(averaged, best, [far_new])
    return score(averaged, best, [far_new_other], inv_pattern)


def solution(mesh):
    in_specs = (
        P(None, "strip", "dict"),
        P("strip", "dict"),
        P(None, "strip", "dict"),
        P(None, ("strip", "dict"), None),
    )
    out_specs = P(None, None, "strip", "dict")
    return jax.shard_map(
        on_device, mesh=mesh, in_specs=in_specs, out_specs=out_specs, check_vma=False
    )
```

time: 118 us -> 82.9 us (0.70)
  waiting for transfers between devices: 29.6 us -> 11.4 us
  between operations: 13.6 us -> 0.25 us
  starting transfers between devices: 16.9 us -> 25.5 us
  Pallas kernels: 51.8 us -> 44.6 us
  local copies, waits for them, and re-layouts: 4.86 us -> 0.03 us
    ppermute x3 -> x2, waiting for transfers between devices: 28.9 us -> 10.6 us  [from_high(): return lax.ppermute(x, axis, [(i + 1, i) for i in range(count - 1)])]
    ppermute x0 -> x10, starting transfers between devices: none -> 13.9 us  [exchange(): return lax.ppermute(x, axis, [(i, i ^ masks[i & 1]) for i in range(count)])]
    pallas_call x4 -> x13, Pallas kernels: 51.8 us -> 44.6 us  [the longest x1 11.7 us: average(): pl.pallas_call(average_kernel, in_specs=[WHOLE] * (9 + len(earlier)), out...]
    ppermute x3 -> x2, starting transfers between devices: 11.8 us -> 7.42 us  [from_low(): return lax.ppermute(x, axis, [(i, i + 1) for i in range(count - 1)])]
    squeeze x1 -> x0, local copies, waits for them, and re-layouts: 2.54 us -> none  [on_device(): bottom = from_high(standard[0], 'strip')]
    unnamed x6 -> x2, local copies, waits for them, and re-layouts: 1.67 us -> 0.01 us
    ppermute x3 -> x2, starting transfers between devices: 5.13 us -> 4.16 us  [from_high(): return lax.ppermute(x, axis, [(i + 1, i) for i in range(count - 1)])]
  transfers between devices with their start and end apart: 7 -> 14, of which waited for: 1 -> 3; matrix products, arithmetic and copies ran while one was open for 3% -> 1% of each run, Pallas kernels for 32% -> 49%
where the time goes in v1:
time: 82.9 us; the launch traced here: 82.5 us
  Pallas kernels  44.6 us (54%)
  starting transfers between devices  25.5 us (31%)
  waiting for transfers between devices  11.4 us (14%)
    ppermute x10, starting transfers between devices, exchange(): return lax.ppermute(x, axis, [(i, i ^ masks[i & 1]) for i in range(count)])  13.9 us
    pallas_call x1, Pallas kernels, average(): pl.pallas_call(average_kernel, in_specs=[WHOLE] * (9 + len(earlier)), out...  11.7 us
    ppermute x2, waiting for transfers between devices, from_high(): return lax.ppermute(x, axis, [(i + 1, i) for i in range(count - 1)])  10.6 us
    pallas_call x4, Pallas kernels, score(): pl.pallas_call(functools.partial(score_kernel, len(pieces)), in_specs=[WH...  10.4 us
    pallas_call x1, Pallas kernels, interior(): pl.pallas_call(interior_kernel, in_specs=[APART, APART, WHOLE], out_specs...  8.35 us
    ppermute x2, starting transfers between devices, from_low(): return lax.ppermute(x, axis, [(i, i + 1) for i in range(count - 1)])  7.42 us
    pallas_call x1, Pallas kernels, border(): pl.pallas_call(border_kernel, in_specs=[APART] * 3, out_specs=(APART, WHO...  6.32 us
    ppermute x2, starting transfers between devices, from_high(): return lax.ppermute(x, axis, [(i + 1, i) for i in range(count - 1)])  4.16 us
  transfers between devices with their start and end apart: 14, of which 3 were waited for; matrix products, arithmetic and copies ran while one was open for 1% of the time, Pallas kernels for 49%

profile of v1, /device:TPU:1, one launch (start us, length us, event | category | flops | bytes accessed | tf_op | source)
XLA Modules:
  0.0 82.5 jit_solution(965357430286782033)
XLA Ops:
  0.0 2.1 %collective-permute-start.1 = (bf16[2,16,3600]{2,1,0:T(8,128)(2,1)}, bf16[2,16,3600]{2,1,0:T(8,128)(2,1)S(1)}, u32[]{:S(2)}, u32[]{:S(2)}) collective-permute-start(bf16[2,16,3600]{2,1,0:T(8,128)(2,1)} %refs_0_.1), channel_id=1, source_target_pairs={{0,8},{4,20},{8,0},{12,28},{16,24},{20,4},{24,16},{28,12},{1,9},{5... | collective-permute-start | bytes 691208 | tf_op jit(solution)/shard_map/ppermute | solution.py:473
  2.1 6.3 %border.1 = (bf16[6,15,240,128]{3,2,1,0:T(8,128)(2,1)}, bf16[3600,128]{1,0:T(8,128)(2,1)S(1)}, bf16[3600,128]{1,0:T(8,128)(2,1)S(1)}, f32[8,128]{1,0:T(8,128)S(1)}) custom-call(bf16[3600,8,128]{2,1,0:T(8,128)(2,1)} %x_hbm.1, s32[8,128]{1,0:T(8,128)} %mask_hbm.1, bf16[3,240,256]{2,1,0:T(8,128)(2,1)} %constant.11.clone.mat_hbm), custom_call_target="tpu_custom_call" | custom-call | flops 1000 | bytes 1000 | tf_op jit(solution)/shard_map/border/pallas_call | solution.py:156
  8.4 1.0 %join.4 = (bf16[2,32,3600]{2,1,0:T(8,128)(2,1)S(1)}, f32[8,128]{1,0:T(8,128)S(1)}) custom-call(bf16[2,16,3600]{2,1,0:T(8,128)(2,1)} %refs_0_.1, bf16[2,16,3600]{2,1,0:T(8,128)(2,1)S(1)} %collective-permute-done.1.refs_1_, f32[8,128]{1,0:T(8,128)S(1)} %get-tuple-element.27.refs_2_), custom_call_target="tpu_custom_call" | custom-call | flops 1000 | bytes 1000 | tf_op jit(solution)/shard_map/join/pallas_call | solution.py:516
  9.4 1.3 %collective-permute-start.6 = (bf16[2,32,3600]{2,1,0:T(8,128)(2,1)S(1)}, bf16[2,32,3600]{2,1,0:T(8,128)(2,1)}, u32[]{:S(2)}, u32[]{:S(2)}) collective-permute-start(bf16[2,32,3600]{2,1,0:T(8,128)(2,1)S(1)} %get-tuple-element.30.refs_0_), channel_id=1, source_target_pairs={{0,16},{4,12},{8,24},{12,4},{16,0},{20,28},{24,8},{28,20},{1,17},{... | collective-permute-start | bytes 1382408 | tf_op jit(solution)/shard_map/ppermute | solution.py:473
  10.7 1.3 %collective-permute-start.3 = (bf16[2,16,3600]{2,1,0:T(8,128)(2,1)}, bf16[2,16,3600]{2,1,0:T(8,128)(2,1)S(1)}, u32[]{:S(2)}, u32[]{:S(2)}) collective-permute-start(bf16[2,16,3600]{2,1,0:T(8,128)(2,1)} %refs_0_.1), channel_id=1, source_target_pairs={{0,1},{1,0},{2,3},{3,2},{4,5},{5,4},{6,7},{7,6},{8,9},{9,8},{10,11... | collective-permute-start | bytes 691208 | tf_op jit(solution)/shard_map/ppermute | solution.py:473
  12.0 2.3 %collective-permute-start.4 = (bf16[2,16,3600]{2,1,0:T(8,128)(2,1)}, bf16[2,16,3600]{2,1,0:T(8,128)(2,1)}, u32[]{:S(2)}, u32[]{:S(2)}) collective-permute-start(bf16[2,16,3600]{2,1,0:T(8,128)(2,1)} %refs_0_.1), channel_id=1, source_target_pairs={{0,2},{1,3},{2,0},{3,1},{4,6},{5,7},{6,4},{7,5},{8,10},{9,11},{10,... | collective-permute-start | bytes 691208 | tf_op jit(solution)/shard_map/ppermute | solution.py:473
  14.3 4.1 %collective-permute-start = (bf16[3600,128]{1,0:T(8,128)(2,1)S(1)}, bf16[3600,128]{1,0:T(8,128)(2,1)S(1)}, u32[]{:S(2)}, u32[]{:S(2)}) collective-permute-start(bf16[3600,128]{1,0:T(8,128)(2,1)S(1)} %get-tuple-element.24.refs_3_), channel_id=1, source_target_pairs={{0,4},{4,8},{8,12},{12,16},{16,20},{20,24},{24,28},{1,5},{5,9},{9,... | collective-permute-start | bytes 2764808 | tf_op jit(solution)/shard_map/ppermute | solution.py:539
  18.3 2.7 %collective-permute-start.2 = (bf16[3600,128]{1,0:T(8,128)(2,1)S(1)}, bf16[3600,128]{1,0:T(8,128)(2,1)}, u32[]{:S(2)}, u32[]{:S(2)}) collective-permute-start(bf16[3600,128]{1,0:T(8,128)(2,1)S(1)} %get-tuple-element.25.refs_1_), channel_id=1, source_target_pairs={{4,0},{8,4},{12,8},{16,12},{20,16},{24,20},{28,24},{5,1},{9,5},{13... | collective-permute-start | bytes 2764808 | tf_op jit(solution)/shard_map/ppermute | solution.py:544
  21.1 8.3 %interior.1 = (bf16[6,3600,128]{2,1,0:T(8,128)(2,1)S(1)}, f32[8,128]{1,0:T(8,128)S(1)}) custom-call(bf16[6,15,240,128]{3,2,1,0:T(8,128)(2,1)} %get-tuple-element.26.xq_hbm, bf16[3,240,256]{2,1,0:T(8,128)(2,1)} %constant.11.clone.mat_hbm, f32[8,128]{1,0:T(8,128)S(1)} %get-tuple-element.28._), custom_call_target="tpu_custom_call" | custom-call | flops 1000 | bytes 1000 | tf_op jit(solution)/shard_map/interior/pallas_call | solution.py:219
  29.4 1.2 %join.5 = (bf16[2,64,3600]{2,1,0:T(8,128)(2,1)S(1)}, f32[8,128]{1,0:T(8,128)S(1)}) custom-call(bf16[2,32,3600]{2,1,0:T(8,128)(2,1)S(1)} %get-tuple-element.30.refs_0_, bf16[2,32,3600]{2,1,0:T(8,128)(2,1)} %collective-permute-done.6.refs_1_, f32[8,128]{1,0:T(8,128)S(1)} %get-tuple-element.31.refs_2_), custom_call_target="tpu_custom_call" | custom-call | flops 1000 | bytes 1000 | tf_op jit(solution)/shard_map/join/pallas_call | solution.py:516
  30.7 1.2 %join.6 = (bf16[2,48,3600]{2,1,0:T(8,128)(2,1)S(1)}, f32[8,128]{1,0:T(8,128)S(1)}) custom-call(bf16[2,16,3600]{2,1,0:T(8,128)(2,1)S(1)} %collective-permute-done.3.refs_0_, bf16[2,16,3600]{2,1,0:T(8,128)(2,1)} %collective-permute-done.4.refs_1_, bf16[2,16,3600]{2,1,0:T(8,128)(2,1)} %collective-permute-done.5.refs_2_, f32[8,128]{1,0:T(8,128)S(1)} %get-tuple-element.32.refs_3_), custom_call_target="tpu_custom_call" | custom-call | flops 1000 | bytes 1000 | tf_op jit(solution)/shard_map/join/pallas_call | solution.py:516
  31.9 1.3 %collective-permute-start.9 = (bf16[2,48,3600]{2,1,0:T(8,128)(2,1)S(1)}, bf16[2,48,3600]{2,1,0:T(8,128)(2,1)S(1)}, u32[]{:S(2)}, u32[]{:S(2)}) collective-permute-start(bf16[2,48,3600]{2,1,0:T(8,128)(2,1)S(1)} %get-tuple-element.37.refs_0_), channel_id=1, source_target_pairs={{0,8},{4,20},{8,0},{12,28},{16,24},{20,4},{24,16},{28,12},{1,9},{5... | collective-permute-start | bytes 2073608 | tf_op jit(solution)/shard_map/ppermute | solution.py:473
  33.5 6.8 %collective-permute-done.2.refs_4_ = bf16[3600,128]{1,0:T(8,128)(2,1)} collective-permute-done((bf16[3600,128]{1,0:T(8,128)(2,1)S(1)}, bf16[3600,128]{1,0:T(8,128)(2,1)}, u32[]{:S(2)}, u32[]{:S(2)}) %collective-permute-start.2) | collective-permute-done | bytes 921632 | tf_op jit(solution)/shard_map/ppermute | solution.py:544
  40.3 4.1 %products.1 = (bf16[16,3600]{1,0:T(8,128)(2,1)S(1)}, bf16[16,3600]{1,0:T(8,128)(2,1)S(1)}, f32[10,8,128]{2,1,0:T(8,128)S(1)}) custom-call(bf16[3600,128]{1,0:T(8,128)(2,1)S(1)} %collective-permute-done.refs_0_, bf16[3600,128]{1,0:T(8,128)(2,1)S(1)} %get-tuple-element.25.refs_1_, bf16[6,3600,128]{2,1,0:T(8,128)(2,1)S(1)} %get-tuple-element.29.refs_2_, ...), custom_call_target="tpu_custom_call" | custom-call | flops 1000 | bytes 1000 | tf_op jit(solution)/shard_map/products/pallas_call | solution.py:290
  44.8 3.5 %collective-permute-start.12 = (bf16[2,96,3600]{2,1,0:T(8,128)(2,1)S(1)}, bf16[2,96,3600]{2,1,0:T(8,128)(2,1)S(1)}, u32[]{:S(2)}, u32[]{:S(2)}) collective-permute-start(bf16[2,96,3600]{2,1,0:T(8,128)(2,1)S(1)} %get-tuple-element.41.refs_0_), channel_id=1, source_target_pairs={{0,16},{4,12},{8,24},{12,4},{16,0},{20,28},{24,8},{28,20},{1,17},{... | collective-permute-start | bytes 4147208 | tf_op jit(solution)/shard_map/ppermute | solution.py:473
  49.3 3.4 %collective-permute-start.7 = (bf16[16,3600]{1,0:T(8,128)(2,1)S(1)}, bf16[16,3600]{1,0:T(8,128)(2,1)S(1)}, u32[]{:S(2)}, u32[]{:S(2)}) collective-permute-start(bf16[16,3600]{1,0:T(8,128)(2,1)S(1)} %get-tuple-element.34), channel_id=1, source_target_pairs={{0,1},{1,2},{2,3},{4,5},{5,6},{6,7},{8,9},{9,10},{10,11},{12,13},{... | collective-permute-start | bytes 345608 | tf_op jit(solution)/shard_map/ppermute | solution.py:539
  52.7 1.5 %collective-permute-start.8 = (bf16[16,3600]{1,0:T(8,128)(2,1)S(1)}, bf16[16,3600]{1,0:T(8,128)(2,1)S(1)}, u32[]{:S(2)}, u32[]{:S(2)}) collective-permute-start(bf16[16,3600]{1,0:T(8,128)(2,1)S(1)} %get-tuple-element.35), channel_id=1, source_target_pairs={{1,0},{2,1},{3,2},{5,4},{6,5},{7,6},{9,8},{10,9},{11,10},{13,12},{... | collective-permute-start | bytes 345608 | tf_op jit(solution)/shard_map/ppermute | solution.py:544
  55.3 3.8 %collective-permute-done.8.refs_6_ = bf16[16,3600]{1,0:T(8,128)(2,1)S(1)} collective-permute-done((bf16[16,3600]{1,0:T(8,128)(2,1)S(1)}, bf16[16,3600]{1,0:T(8,128)(2,1)S(1)}, u32[]{:S(2)}, u32[]{:S(2)}) %collective-permute-start.8) | collective-permute-done | bytes 115232 | tf_op jit(solution)/shard_map/ppermute | solution.py:544
  59.1 11.7 %average.1 = (bf16[8,3600,128]{2,1,0:T(8,128)(2,1)S(1)}, f32[8,128]{1,0:T(8,128)S(1)}) custom-call(bf16[3600,128]{1,0:T(8,128)(2,1)S(1)} %collective-permute-done.refs_0_, bf16[3600,128]{1,0:T(8,128)(2,1)S(1)} %get-tuple-element.25.refs_1_, bf16[6,3600,128]{2,1,0:T(8,128)(2,1)S(1)} %get-tuple-element.29.refs_2_, ...), custom_call_target="tpu_custom_call" | custom-call | flops 1000 | bytes 1000 | tf_op jit(solution)/shard_map/average/pallas_call | solution.py:389
  70.8 2.3 %score.4.best_ref.refs_1_ = f32[2,4,8,8,128]{4,3,2,1,0:T(8,128)S(1)} custom-call(bf16[8,3600,128]{2,1,0:T(8,128)(2,1)S(1)} %get-tuple-element.39.a_ref, f32[2,4,8,8,128]{4,3,2,1,0:T(8,128)S(1)} %broadcast_in_dim.2.best_ref, bf16[2,64,3600]{2,1,0:T(8,128)(2,1)S(1)} %get-tuple-element.40.refs_0_, bf16[2,64,3600]{2,1,0:T(8,128)(2,1)S(1)} %collective-permute-done.10.refs_1_), custom_call_target="tpu_custom_call" | custom-call | flops 1000 | bytes 1000 | tf_op jit(solution)/shard_map/score/pallas_call | solution.py:460
  73.2 1.2 %collective-permute-start.13 = (bf16[2,96,3600]{2,1,0:T(8,128)(2,1)S(1)}, bf16[2,96,3600]{2,1,0:T(8,128)(2,1)S(1)}, u32[]{:S(2)}, u32[]{:S(2)}) collective-permute-start(bf16[2,96,3600]{2,1,0:T(8,128)(2,1)S(1)} %hold.1.refs_0_), channel_id=1, source_target_pairs={{0,4},{4,0},{8,12},{12,8},{16,20},{20,16},{24,28},{28,24},{1,5},{5... | collective-permute-start | bytes 4147208 | tf_op jit(solution)/shard_map/ppermute | solution.py:473
  74.4 3.7 %score.5.best_ref = f32[2,4,8,8,128]{4,3,2,1,0:T(8,128)S(1)} custom-call(bf16[8,3600,128]{2,1,0:T(8,128)(2,1)S(1)} %get-tuple-element.39.a_ref, f32[2,4,8,8,128]{4,3,2,1,0:T(8,128)S(1)} %score.4.best_ref.refs_1_, bf16[2,96,3600]{2,1,0:T(8,128)(2,1)S(1)} %get-tuple-element.41.refs_0_, bf16[2,96,3600]{2,1,0:T(8,128)(2,1)S(1)} %collective-permute-done.11.refs_1_), custom_call_target="tpu_custom_call" | custom-call | flops 1000 | bytes 1000 | tf_op jit(solution)/shard_map/score/pallas_call | solution.py:460
  78.1 1.9 %score.6.best_ref = f32[2,4,8,8,128]{4,3,2,1,0:T(8,128)S(1)} custom-call(bf16[8,3600,128]{2,1,0:T(8,128)(2,1)S(1)} %get-tuple-element.39.a_ref, f32[2,4,8,8,128]{4,3,2,1,0:T(8,128)S(1)} %score.5.best_ref, bf16[2,96,3600]{2,1,0:T(8,128)(2,1)S(1)} %hold.1.refs_0_), custom_call_target="tpu_custom_call" | custom-call | flops 1000 | bytes 1000 | tf_op jit(solution)/shard_map/score/pallas_call | solution.py:460
  80.0 2.5 %score.7 = f32[2,4,8,128]{3,2,1,0:T(8,128)} custom-call(bf16[8,3600,128]{2,1,0:T(8,128)(2,1)S(1)} %get-tuple-element.39.a_ref, f32[2,4,8,8,128]{4,3,2,1,0:T(8,128)S(1)} %score.6.best_ref, bf16[2,96,3600]{2,1,0:T(8,128)(2,1)S(1)} %collective-permute-done.13.refs_0_, f32[8,128]{1,0:T(8,128)S(1)} %get-tuple-element.42.refs_1_), custom_call_target="tpu_custom_call" | custom-call | flops 1000 | bytes 1000 | tf_op jit(solution)/shard_map/score/pallas_call | solution.py:460
  (33 shorter events, 2.9 us)
Async XLA Ops:
  0.0 8.4 %collective-permute-start.1 = (bf16[2,16,3600]{2,1,0:T(8,128)(2,1)}, bf16[2,16,3600]{2,1,0:T(8,128)(2,1)S(1)}, u32[]{:S(2)}, u32[]{:S(2)}) collective-permute-start(bf16[2,16,3600]{2,1,0:T(8,128)(2,1)} %refs_0_.1), channel_id=1, source_target_pairs={{0,8},{4,20},{8,0},{12,28},{16,24},{20,4},{24,16},{28,12},{1,9},{5... | collective-permute-start | bytes 691208 | tf_op jit(solution)/shard_map/ppermute | solution.py:473
  9.4 9.0 %collective-permute-start.6 = (bf16[2,32,3600]{2,1,0:T(8,128)(2,1)S(1)}, bf16[2,32,3600]{2,1,0:T(8,128)(2,1)}, u32[]{:S(2)}, u32[]{:S(2)}) collective-permute-start(bf16[2,32,3600]{2,1,0:T(8,128)(2,1)S(1)} %get-tuple-element.30.refs_0_), channel_id=1, source_target_pairs={{0,16},{4,12},{8,24},{12,4},{16,0},{20,28},{24,8},{28,20},{1,17},{... | collective-permute-start | bytes 1382408 | tf_op jit(solution)/shard_map/ppermute | solution.py:473
  10.7 20.0 %collective-permute-start.3 = (bf16[2,16,3600]{2,1,0:T(8,128)(2,1)}, bf16[2,16,3600]{2,1,0:T(8,128)(2,1)S(1)}, u32[]{:S(2)}, u32[]{:S(2)}) collective-permute-start(bf16[2,16,3600]{2,1,0:T(8,128)(2,1)} %refs_0_.1), channel_id=1, source_target_pairs={{0,1},{1,0},{2,3},{3,2},{4,5},{5,4},{6,7},{7,6},{8,9},{9,8},{10,11... | collective-permute-start | bytes 691208 | tf_op jit(solution)/shard_map/ppermute | solution.py:473
  12.0 18.7 %collective-permute-start.4 = (bf16[2,16,3600]{2,1,0:T(8,128)(2,1)}, bf16[2,16,3600]{2,1,0:T(8,128)(2,1)}, u32[]{:S(2)}, u32[]{:S(2)}) collective-permute-start(bf16[2,16,3600]{2,1,0:T(8,128)(2,1)} %refs_0_.1), channel_id=1, source_target_pairs={{0,2},{1,3},{2,0},{3,1},{4,6},{5,7},{6,4},{7,5},{8,10},{9,11},{10,... | collective-permute-start | bytes 691208 | tf_op jit(solution)/shard_map/ppermute | solution.py:473
  14.3 16.4 %collective-permute-start.5 = (bf16[2,16,3600]{2,1,0:T(8,128)(2,1)}, bf16[2,16,3600]{2,1,0:T(8,128)(2,1)}, u32[]{:S(2)}, u32[]{:S(2)}) collective-permute-start(bf16[2,16,3600]{2,1,0:T(8,128)(2,1)} %refs_0_.1), channel_id=1, source_target_pairs={{0,3},{1,2},{2,1},{3,0},{4,7},{5,6},{6,5},{7,4},{8,11},{9,10},{10,... | collective-permute-start | bytes 691208 | tf_op jit(solution)/shard_map/ppermute | solution.py:473
  14.3 19.2 %collective-permute-start = (bf16[3600,128]{1,0:T(8,128)(2,1)S(1)}, bf16[3600,128]{1,0:T(8,128)(2,1)S(1)}, u32[]{:S(2)}, u32[]{:S(2)}) collective-permute-start(bf16[3600,128]{1,0:T(8,128)(2,1)S(1)} %get-tuple-element.24.refs_3_), channel_id=1, source_target_pairs={{0,4},{4,8},{8,12},{12,16},{16,20},{20,24},{24,28},{1,5},{5,9},{9,... | collective-permute-start | bytes 2764808 | tf_op jit(solution)/shard_map/ppermute | solution.py:539
  18.3 21.9 %collective-permute-start.2 = (bf16[3600,128]{1,0:T(8,128)(2,1)S(1)}, bf16[3600,128]{1,0:T(8,128)(2,1)}, u32[]{:S(2)}, u32[]{:S(2)}) collective-permute-start(bf16[3600,128]{1,0:T(8,128)(2,1)S(1)} %get-tuple-element.25.refs_1_), channel_id=1, source_target_pairs={{4,0},{8,4},{12,8},{16,12},{20,16},{24,20},{28,24},{5,1},{9,5},{13... | collective-permute-start | bytes 2764808 | tf_op jit(solution)/shard_map/ppermute | solution.py:544
  31.9 12.5 %collective-permute-start.9 = (bf16[2,48,3600]{2,1,0:T(8,128)(2,1)S(1)}, bf16[2,48,3600]{2,1,0:T(8,128)(2,1)S(1)}, u32[]{:S(2)}, u32[]{:S(2)}) collective-permute-start(bf16[2,48,3600]{2,1,0:T(8,128)(2,1)S(1)} %get-tuple-element.37.refs_0_), channel_id=1, source_target_pairs={{0,8},{4,20},{8,0},{12,28},{16,24},{20,4},{24,16},{28,12},{1,9},{5... | collective-permute-start | bytes 2073608 | tf_op jit(solution)/shard_map/ppermute | solution.py:473
  44.4 9.8 %copy-start = (s32[8,8,128]{2,1,0:T(8,128)S(1)}, s32[8,8,128]{2,1,0:T(8,128)}, u32[]{:S(2)}) copy-start(s32[8,8,128]{2,1,0:T(8,128)} %param.7) | copy-start | bytes 98308
  44.8 28.4 %collective-permute-start.12 = (bf16[2,96,3600]{2,1,0:T(8,128)(2,1)S(1)}, bf16[2,96,3600]{2,1,0:T(8,128)(2,1)S(1)}, u32[]{:S(2)}, u32[]{:S(2)}) collective-permute-start(bf16[2,96,3600]{2,1,0:T(8,128)(2,1)S(1)} %get-tuple-element.41.refs_0_), channel_id=1, source_target_pairs={{0,16},{4,12},{8,24},{12,4},{16,0},{20,28},{24,8},{28,20},{1,17},{... | collective-permute-start | bytes 4147208 | tf_op jit(solution)/shard_map/ppermute | solution.py:473
  48.3 22.5 %collective-permute-start.10 = (bf16[2,64,3600]{2,1,0:T(8,128)(2,1)S(1)}, bf16[2,64,3600]{2,1,0:T(8,128)(2,1)S(1)}, u32[]{:S(2)}, u32[]{:S(2)}) collective-permute-start(bf16[2,64,3600]{2,1,0:T(8,128)(2,1)S(1)} %get-tuple-element.40.refs_0_), channel_id=1, source_target_pairs={{0,4},{4,0},{8,12},{12,8},{16,20},{20,16},{24,28},{28,24},{1,5},{5... | collective-permute-start | bytes 2764808 | tf_op jit(solution)/shard_map/ppermute | solution.py:473
  49.3 6.0 %collective-permute-start.7 = (bf16[16,3600]{1,0:T(8,128)(2,1)S(1)}, bf16[16,3600]{1,0:T(8,128)(2,1)S(1)}, u32[]{:S(2)}, u32[]{:S(2)}) collective-permute-start(bf16[16,3600]{1,0:T(8,128)(2,1)S(1)} %get-tuple-element.34), channel_id=1, source_target_pairs={{0,1},{1,2},{2,3},{4,5},{5,6},{6,7},{8,9},{9,10},{10,11},{12,13},{... | collective-permute-start | bytes 345608 | tf_op jit(solution)/shard_map/ppermute | solution.py:539
  52.7 6.4 %collective-permute-start.8 = (bf16[16,3600]{1,0:T(8,128)(2,1)S(1)}, bf16[16,3600]{1,0:T(8,128)(2,1)S(1)}, u32[]{:S(2)}, u32[]{:S(2)}) collective-permute-start(bf16[16,3600]{1,0:T(8,128)(2,1)S(1)} %get-tuple-element.35), channel_id=1, source_target_pairs={{1,0},{2,1},{3,2},{5,4},{6,5},{7,6},{9,8},{10,9},{11,10},{13,12},{... | collective-permute-start | bytes 345608 | tf_op jit(solution)/shard_map/ppermute | solution.py:544
  54.2 20.2 %collective-permute-start.11 = (bf16[2,96,3600]{2,1,0:T(8,128)(2,1)S(1)}, bf16[2,96,3600]{2,1,0:T(8,128)(2,1)S(1)}, u32[]{:S(2)}, u32[]{:S(2)}) collective-permute-start(bf16[2,96,3600]{2,1,0:T(8,128)(2,1)S(1)} %get-tuple-element.41.refs_0_), channel_id=1, source_target_pairs={{0,4},{4,0},{8,12},{12,8},{16,20},{20,16},{24,28},{28,24},{1,5},{5... | collective-permute-start | bytes 4147208 | tf_op jit(solution)/shard_map/ppermute | solution.py:473
  73.2 6.7 %collective-permute-start.13 = (bf16[2,96,3600]{2,1,0:T(8,128)(2,1)S(1)}, bf16[2,96,3600]{2,1,0:T(8,128)(2,1)S(1)}, u32[]{:S(2)}, u32[]{:S(2)}) collective-permute-start(bf16[2,96,3600]{2,1,0:T(8,128)(2,1)S(1)} %hold.1.refs_0_), channel_id=1, source_target_pairs={{0,4},{4,0},{8,12},{12,8},{16,20},{20,16},{24,28},{28,24},{1,5},{5... | collective-permute-start | bytes 4147208 | tf_op jit(solution)/shard_map/ppermute | solution.py:473

commit v2 on v1

--- a/solution.py
+++ b/solution.py
@@ -178,47 +178,47 @@
     )(in_hbm(patterns), in_hbm(scan_mask), in_hbm(matrices))
 
 
-def interior_kernel(xq_hbm, mat_hbm, _, s_ref, token, mat_ref, xq, half, corr, sq, sems):
+def interior_kernel(xq_hbm, mat_hbm, *refs):
+    s_ref, token, mat_ref, xq, half, corr, sq, sems = refs[-8:]
     mark(token)
     pairs = s_ref.shape[0] // 2
     matrices = pltpu.make_async_copy(mat_hbm, mat_ref, sems.at[2])
 
-    def fetch(i, slot):
+    def fetch(i):
+        slot = i % 2
         return pltpu.make_async_copy(xq_hbm.at[pl.ds(2 * i, 2)], xq.at[slot], sems.at[slot])
 
-    fetch(0, 0).start()
+    fetch(0).start()
     matrices.start()
+    if pairs > 1:
+        fetch(1).start()
     matrices.wait()
 
-    def pair(i, carry):
-        slot = lax.rem(i, 2)
-        fetch(i, slot).wait()
-
-        @pl.when(i + 1 < pairs)
-        def _():
-            fetch(i + 1, 1 - slot).start()
-
+    def work(source, at):
         def both(quad, span):
-            return jnp.concatenate([xq[slot, 0, quad, span, :], xq[slot, 1, quad, span, :]], axis=1)
+            return jnp.concatenate([source[0, quad, span, :], source[1, quad, span, :]], axis=1)
 
         def store(side):
             def put(span, value):
-                s_ref[2 * i + side, span, :] = value
+                s_ref[at + side, span, :] = value
 
             return put
 
         standard_rows(both, mat_ref, half, corr, sq, [store(0), store(1)])
-        return carry
-
-    lax.fori_loop(0, pairs, pair, 0)
-
-
-def interior(xq, matrices, earlier):
+
+    for i in range(pairs):
+        fetch(i).wait()
+        work(xq.at[i % 2], 2 * i)
+        if i + 2 < pairs:
+            fetch(i + 2).start()
+
+
+def interior(xq, matrices, *earlier):
     rows, _, _, cols = xq.shape
     pixels = GROUPS * CHUNK
     return pl.pallas_call(
         interior_kernel,
-        in_specs=[APART, APART, WHOLE],
+        in_specs=[APART, APART] + [WHOLE] * len(earlier),
         out_specs=(WHOLE, WHOLE),
         out_shape=(pltpu.VMEM((rows, pixels, cols), jnp.bfloat16), TOKEN),
         scratch_shapes=[
@@ -230,7 +230,7 @@
         compiler_params=pltpu.CompilerParams(vmem_limit_bytes=16 * MIB),
         cost_estimate=SHORT,
         name="interior",
-    )(in_hbm(xq), in_hbm(matrices), earlier)
+    )(in_hbm(xq), in_hbm(matrices), *earlier)
 
 
 def row_of(refs, rows):
@@ -299,7 +299,7 @@
 
 
 def average_kernel(*refs):
-    left_ref, right_ref, dot_ref, usable_ref = refs[5:9]
+    left_ref, right_ref, own_left_ref, own_right_ref, dot_ref, usable_ref = refs[5:11]
     a_ref, inv_ref, sides, weights = refs[-4:]
     rows, pixels, cols = a_ref.shape
     row = row_of(refs[:5], rows)
@@ -308,13 +308,19 @@
     at_lane = lax.broadcasted_iota(jnp.int32, (cols, cols), 1)
     lane = lax.broadcasted_iota(jnp.int32, (1, cols), 1)
 
-    side = jnp.concatenate([left_ref[...], right_ref[...]], axis=0)
-    side32 = side.astype(f32)
-    side_norm = jnp.sum(side32 * side32, axis=1, keepdims=True)
-    pad = jnp.concatenate([side32, jnp.zeros((cols - SIDES, pixels), f32)], axis=0)
+    pad = jnp.zeros((LANES, cols - SIDES), f32)
     for start in range(0, pixels, LANES):
         width = min(LANES, pixels - start)
-        sides[pl.ds(start, width), :] = pad[:, start : start + width].T.astype(jnp.bfloat16)
+        span = slice(start, start + width)
+        piece = jnp.concatenate([left_ref[:, span], right_ref[:, span]], axis=0).astype(f32)
+        sides[span, :] = jnp.concatenate([piece.T, pad[:width]], axis=1).astype(jnp.bfloat16)
+
+    meet = []
+    for own, halo in ((own_left_ref, left_ref), (own_right_ref, right_ref)):
+        both = jnp.concatenate([own[...], halo[...]], axis=0)
+        meet.append(
+            lax.dot_general(both, halo[...], (((1,), (1,)), ((), ())), preferred_element_type=f32)
+        )
 
     def shifted(vector, dc):
         if dc == 0:
@@ -325,7 +331,6 @@
         return dot_ref[r + 1, pl.ds(k, 1), :]
 
     for r in range(rows):
-        to_side = jnp.dot(side, row(r)[...], preferred_element_type=f32)
         weight = {}
         slot = 0
         total = jnp.ones((1, cols), f32)
@@ -341,10 +346,11 @@
                     dot = kept(r, 1) if dc == -1 else shifted(kept(r, 1), 1)
                 other = shifted(kept(r + dr, 0), dc)
                 if dc != 0:
-                    k = r + dr + 1 + (0 if dc < 0 else 16)
+                    k, near = r + dr + 1, meet[0 if dc < 0 else 1]
                     end = 0 if dc < 0 else cols - 1
-                    dot = jnp.where(lane == end, to_side[k : k + 1, :], dot)
-                    other = jnp.where(lane == end, side_norm[k : k + 1, :], other)
+                    half = SIDES // 2
+                    dot = jnp.where(lane == end, near[r + 1 : r + 2, k : k + 1], dot)
+                    other = jnp.where(lane == end, near[half + k : half + k + 1, k : k + 1], other)
                 distance = jnp.maximum(kept(r, 0) + other - 2.0 * dot, 0.0) / pixels
                 weight[dr, dc] = usable_ref[slot, pl.ds(r, 1), :] * jnp.exp(-distance / nlpar_scale)
                 total = total + weight[dr, dc]
@@ -383,12 +389,12 @@
         inv_ref[pl.ds(r, 1), :] = 1.0 / jnp.sqrt(energy + epsilon)
 
 
-def average(block, left, right, dots, usable, *earlier):
+def average(block, left, right, own_left, own_right, dots, usable, *earlier):
     rows = block[2].shape[0] + 2
     pixels, cols = block[0].shape
     return pl.pallas_call(
         average_kernel,
-        in_specs=[WHOLE] * (9 + len(earlier)),
+        in_specs=[WHOLE] * (11 + len(earlier)),
         out_specs=(WHOLE, WHOLE),
         out_shape=(
             pltpu.VMEM((rows, pixels, cols), jnp.bfloat16),
@@ -401,7 +407,7 @@
         compiler_params=pltpu.CompilerParams(vmem_limit_bytes=8 * MIB),
         cost_estimate=SHORT,
         name="average",
-    )(*map(on_chip, block), left, right, dots, usable, *earlier)
+    )(*map(on_chip, block), left, right, own_left, own_right, dots, usable, *earlier)
 
 
 def insert(best, new):
@@ -529,6 +535,10 @@
     return power_of_two(strip) and power_of_two(line) and strip > 2 and line > 1
 
 
+def line_masks(line):
+    return [line - 1] + [1 << i for i in range(line.bit_length() - 2)]
+
+
 def strip_masks(strip):
     bits = [1 << i for i in range(1, strip.bit_length() - 1)]
     return list(zip(bits, reversed(bits)))
@@ -570,20 +580,27 @@
     best = jnp.full((dictionary.shape[0], TOP, rows, 8, cols), -jnp.inf, jnp.float32)
     if not alone:
         ways = strip_masks(strip)
-        near = dictionary
-        near_new = exchange(near, "strip", ways[0])
-        far = [exchange(dictionary, "dict", (mask, mask)) for mask in range(1, line)]
+        near = held = dictionary
+        mirrored, *masks = line_masks(line)
+        far = [exchange(held, "dict", (mirrored, mirrored))]
+        plain = [(even, even) for even, _ in ways]
+        near_new = exchange(near, "strip", plain[0])
 
     xq, first, last, bordered = border(patterns, scan_mask, matrices)
     above = from_low(last, "strip")
     below = from_high(first, "strip")
-    done = bordered
+    joined = [bordered]
     if not alone:
-        for way in ways[1:]:
+        for mask in masks:
+            held, done = join([held, far[-1]], bordered)
+            far.append(exchange(held, "dict", (mask, mask)))
+            joined.append(done)
+        for way in plain[1:]:
             near, done = join([near, near_new], bordered)
             near_new = exchange(near, "strip", way)
-
-    middle, filled = interior(xq, matrices, done)
+            joined.append(done)
+
+    middle, filled = interior(xq, matrices, *joined)
     block = (above, first, middle, last, below)
     joined = [filled]
     if not alone:
@@ -599,19 +616,19 @@
     joined = []
     if not alone:
         for way in ways[1:]:
-            far, done = join([far, far_new], dots)
+            far, done = join([far, far_new], left, right)
             far_new = exchange(far, "strip", way)
         joined = [done]
         far_other = exchange(far, "strip", (1, 1))
 
-    averaged, inv_pattern = average(block, left, right, dots, usable, *joined)
+    averaged, inv_pattern = average(block, left, right, own_left, own_right, dots, usable, *joined)
     if alone:
         whole = lax.all_gather(dictionary, ("strip", "dict"), axis=1, tiled=True)
         return score(averaged, best, [whole], inv_pattern)
     best = score(averaged, best, [near, near_other])
+    best = score(averaged, best, [far, far_other])
     far_new = hold(far_new, best)
     far_new_other = exchange(far_new, "strip", (1, 1))
-    best = score(averaged, best, [far, far_other])
     best = score(averaged, best, [far_new])
     return score(averaged, best, [far_new_other], inv_pattern)
 

time: 82.9 us -> 80.6 us (0.972)
  starting transfers between devices: 25.5 us -> 21.8 us
  waiting for transfers between devices: 11.4 us -> 14.3 us
  Pallas kernels: 44.6 us -> 42.9 us
    ppermute x2, starting transfers between devices: 7.42 us -> 5.41 us  [from_low(): return lax.ppermute(x, axis, [(i, i + 1) for i in range(count - 1)])]
    pallas_call x2, Pallas kernels: 20 us -> 18 us  [the longest x1 9.67 us: average(): pl.pallas_call(average_kernel, in_specs=[WHOLE] * (11 + len(earlier)), ou...]
    ppermute x2, waiting for transfers between devices: 10.6 us -> 12.3 us  [from_high(): return lax.ppermute(x, axis, [(i + 1, i) for i in range(count - 1)])]
    ppermute x10 -> x9, waiting for transfers between devices: 0.03 us -> 1.54 us  [exchange(): return lax.ppermute(x, axis, [(i, i ^ masks[i & 1]) for i in range(count)])]
    ppermute x10 -> x9, starting transfers between devices: 13.9 us -> 13 us  [exchange(): return lax.ppermute(x, axis, [(i, i ^ masks[i & 1]) for i in range(count)])]
    pallas_call x4 -> x5, Pallas kernels: 3.74 us -> 4.08 us  [join(): pl.pallas_call(functools.partial(join_kernel, len(parts)), in_specs=[APAR...]
  transfers between devices with their start and end apart: 14 -> 13, of which waited for: 3 -> 5; matrix products, arithmetic and copies ran while one was open for 1% -> 1% of each run, Pallas kernels for 49% -> 50%
where the time goes in v2:
time: 80.6 us; the launch traced here: 79.9 us
  Pallas kernels  42.9 us (53%)
  starting transfers between devices  21.8 us (27%)
  waiting for transfers between devices  14.3 us (18%)
    ppermute x9, starting transfers between devices, exchange(): return lax.ppermute(x, axis, [(i, i ^ masks[i & 1]) for i in range(count)])  13 us
    ppermute x2, waiting for transfers between devices, from_high(): return lax.ppermute(x, axis, [(i + 1, i) for i in range(count - 1)])  12.3 us
    pallas_call x4, Pallas kernels, score(): pl.pallas_call(functools.partial(score_kernel, len(pieces)), in_specs=[WH...  10.2 us
    pallas_call x1, Pallas kernels, average(): pl.pallas_call(average_kernel, in_specs=[WHOLE] * (11 + len(earlier)), ou...  9.67 us
    pallas_call x1, Pallas kernels, interior(): pl.pallas_call(interior_kernel, in_specs=[APART, APART] + [WHOLE] * len(e...  8.36 us
    pallas_call x1, Pallas kernels, border(): pl.pallas_call(border_kernel, in_specs=[APART] * 3, out_specs=(APART, WHO...  6.34 us
    ppermute x2, starting transfers between devices, from_low(): return lax.ppermute(x, axis, [(i, i + 1) for i in range(count - 1)])  5.41 us
    pallas_call x1, Pallas kernels, products(): pl.pallas_call(products_kernel, in_specs=[WHOLE] * (5 + len(earlier)), ou...  4.2 us
  transfers between devices with their start and end apart: 13, of which 5 were waited for; matrix products, arithmetic and copies ran while one was open for 1% of the time, Pallas kernels for 50%

profile of v2, /device:TPU:1, one launch (start us, length us, event | category | flops | bytes accessed | tf_op | source)
XLA Modules:
  0.0 79.9 jit_solution(1936829853145436244)
XLA Ops:
  0.0 2.0 %collective-permute-start.2 = (bf16[2,16,3600]{2,1,0:T(8,128)(2,1)}, bf16[2,16,3600]{2,1,0:T(8,128)(2,1)S(1)}, u32[]{:S(2)}, u32[]{:S(2)}) collective-permute-start(bf16[2,16,3600]{2,1,0:T(8,128)(2,1)} %refs_0_.3), channel_id=1, source_target_pairs={{0,8},{4,12},{8,0},{12,4},{16,24},{20,28},{24,16},{28,20},{1,9},{5... | collective-permute-start | bytes 691208 | tf_op jit(solution)/shard_map/ppermute | solution.py:479
  2.0 3.3 %collective-permute-start.1 = (bf16[2,16,3600]{2,1,0:T(8,128)(2,1)}, bf16[2,16,3600]{2,1,0:T(8,128)(2,1)S(1)}, u32[]{:S(2)}, u32[]{:S(2)}) collective-permute-start(bf16[2,16,3600]{2,1,0:T(8,128)(2,1)} %refs_0_.3), channel_id=1, source_target_pairs={{0,3},{1,2},{2,1},{3,0},{4,7},{5,6},{6,5},{7,4},{8,11},{9,10},{10,... | collective-permute-start | bytes 691208 | tf_op jit(solution)/shard_map/ppermute | solution.py:479
  5.4 6.3 %border.1 = (bf16[6,15,240,128]{3,2,1,0:T(8,128)(2,1)}, bf16[3600,128]{1,0:T(8,128)(2,1)S(1)}, bf16[3600,128]{1,0:T(8,128)(2,1)S(1)}, f32[8,128]{1,0:T(8,128)S(1)}) custom-call(bf16[3600,8,128]{2,1,0:T(8,128)(2,1)} %x_hbm.1, s32[8,128]{1,0:T(8,128)} %mask_hbm.1, bf16[3,240,256]{2,1,0:T(8,128)(2,1)} %constant.11.clone.mat_hbm), custom_call_target="tpu_custom_call" | custom-call | flops 1000 | bytes 1000 | tf_op jit(solution)/shard_map/border/pallas_call | solution.py:156
  12.1 1.3 %collective-permute-start.5 = (bf16[2,32,3600]{2,1,0:T(8,128)(2,1)S(1)}, bf16[2,32,3600]{2,1,0:T(8,128)(2,1)}, u32[]{:S(2)}, u32[]{:S(2)}) collective-permute-start(bf16[2,32,3600]{2,1,0:T(8,128)(2,1)S(1)} %get-tuple-element.34.refs_0_), channel_id=1, source_target_pairs={{0,16},{4,20},{8,24},{12,28},{16,0},{20,4},{24,8},{28,12},{1,17},{... | collective-permute-start | bytes 1382408 | tf_op jit(solution)/shard_map/ppermute | solution.py:479
  13.4 0.8 %join.5 = (bf16[2,32,3600]{2,1,0:T(8,128)(2,1)}, f32[8,128]{1,0:T(8,128)S(1)}) custom-call(bf16[2,16,3600]{2,1,0:T(8,128)(2,1)S(1)} %copy-done, bf16[2,16,3600]{2,1,0:T(8,128)(2,1)S(1)} %collective-permute-done.1.refs_1_.refs_0_, f32[8,128]{1,0:T(8,128)S(1)} %get-tuple-element.29.refs_2_.refs_0_), custom_call_target="tpu_custom_call" | custom-call | flops 1000 | bytes 1000 | tf_op jit(solution)/shard_map/join/pallas_call | solution.py:522
  14.2 2.1 %collective-permute-start.4 = (bf16[2,32,3600]{2,1,0:T(8,128)(2,1)}, bf16[2,32,3600]{2,1,0:T(8,128)(2,1)}, u32[]{:S(2)}, u32[]{:S(2)}) collective-permute-start(bf16[2,32,3600]{2,1,0:T(8,128)(2,1)} %get-tuple-element.33), channel_id=1, source_target_pairs={{0,1},{1,0},{2,3},{3,2},{4,5},{5,4},{6,7},{7,6},{8,9},{9,8},{10,11... | collective-permute-start | bytes 1382408 | tf_op jit(solution)/shard_map/ppermute | solution.py:479
  16.3 3.7 %collective-permute-start = (bf16[3600,128]{1,0:T(8,128)(2,1)S(1)}, bf16[3600,128]{1,0:T(8,128)(2,1)S(1)}, u32[]{:S(2)}, u32[]{:S(2)}) collective-permute-start(bf16[3600,128]{1,0:T(8,128)(2,1)S(1)} %get-tuple-element.26.refs_3_), channel_id=1, source_target_pairs={{0,4},{4,8},{8,12},{12,16},{16,20},{20,24},{24,28},{1,5},{5,9},{9,... | collective-permute-start | bytes 2764808 | tf_op jit(solution)/shard_map/ppermute | solution.py:549
  20.0 2.1 %collective-permute-start.3 = (bf16[3600,128]{1,0:T(8,128)(2,1)S(1)}, bf16[3600,128]{1,0:T(8,128)(2,1)}, u32[]{:S(2)}, u32[]{:S(2)}) collective-permute-start(bf16[3600,128]{1,0:T(8,128)(2,1)S(1)} %get-tuple-element.27.refs_1_), channel_id=1, source_target_pairs={{4,0},{8,4},{12,8},{16,12},{20,16},{24,20},{28,24},{5,1},{9,5},{13... | collective-permute-start | bytes 2764808 | tf_op jit(solution)/shard_map/ppermute | solution.py:554
  22.2 8.4 %interior.1 = (bf16[6,3600,128]{2,1,0:T(8,128)(2,1)S(1)}, f32[8,128]{1,0:T(8,128)S(1)}) custom-call(bf16[6,15,240,128]{3,2,1,0:T(8,128)(2,1)} %get-tuple-element.28.xq_hbm, bf16[3,240,256]{2,1,0:T(8,128)(2,1)} %constant.11.clone.mat_hbm, f32[8,128]{1,0:T(8,128)S(1)} %get-tuple-element.29.refs_2_.refs_0_, f32[8,128]{1,0:T(8,128)S(1)} %get-tuple-element.30.refs_1_, ...), custom_call_target="tpu_custom_call" | custom-call | flops 1000 | bytes 1000 | tf_op jit(solution)/shard_map/interior/pallas_call | solution.py:219
  30.6 1.2 %join.7 = (bf16[2,64,3600]{2,1,0:T(8,128)(2,1)S(1)}, f32[8,128]{1,0:T(8,128)S(1)}) custom-call(bf16[2,32,3600]{2,1,0:T(8,128)(2,1)S(1)} %get-tuple-element.34.refs_0_, bf16[2,32,3600]{2,1,0:T(8,128)(2,1)} %collective-permute-done.5.refs_1_, f32[8,128]{1,0:T(8,128)S(1)} %get-tuple-element.35.refs_2_), custom_call_target="tpu_custom_call" | custom-call | flops 1000 | bytes 1000 | tf_op jit(solution)/shard_map/join/pallas_call | solution.py:522
  31.8 1.2 %join.8 = (bf16[2,48,3600]{2,1,0:T(8,128)(2,1)S(1)}, f32[8,128]{1,0:T(8,128)S(1)}) custom-call(bf16[2,16,3600]{2,1,0:T(8,128)(2,1)S(1)} %collective-permute-done.1.refs_1_.refs_0_, bf16[2,32,3600]{2,1,0:T(8,128)(2,1)} %collective-permute-done.4.refs_1_, f32[8,128]{1,0:T(8,128)S(1)} %get-tuple-element.36.refs_2_), custom_call_target="tpu_custom_call" | custom-call | flops 1000 | bytes 1000 | tf_op jit(solution)/shard_map/join/pallas_call | solution.py:522
  33.0 1.3 %collective-permute-start.8 = (bf16[2,48,3600]{2,1,0:T(8,128)(2,1)S(1)}, bf16[2,48,3600]{2,1,0:T(8,128)(2,1)S(1)}, u32[]{:S(2)}, u32[]{:S(2)}) collective-permute-start(bf16[2,48,3600]{2,1,0:T(8,128)(2,1)S(1)} %get-tuple-element.41.refs_0_), channel_id=1, source_target_pairs={{0,8},{4,20},{8,0},{12,28},{16,24},{20,4},{24,16},{28,12},{1,9},{5... | collective-permute-start | bytes 2073608 | tf_op jit(solution)/shard_map/ppermute | solution.py:479
  34.5 8.6 %collective-permute-done.3.refs_4_ = bf16[3600,128]{1,0:T(8,128)(2,1)} collective-permute-done((bf16[3600,128]{1,0:T(8,128)(2,1)S(1)}, bf16[3600,128]{1,0:T(8,128)(2,1)}, u32[]{:S(2)}, u32[]{:S(2)}) %collective-permute-start.3) | collective-permute-done | bytes 921632 | tf_op jit(solution)/shard_map/ppermute | solution.py:554
  43.0 4.2 %products.1 = (bf16[16,3600]{1,0:T(8,128)(2,1)S(1)}, bf16[16,3600]{1,0:T(8,128)(2,1)S(1)}, f32[10,8,128]{2,1,0:T(8,128)S(1)}) custom-call(bf16[3600,128]{1,0:T(8,128)(2,1)S(1)} %collective-permute-done.refs_0_, bf16[3600,128]{1,0:T(8,128)(2,1)S(1)} %get-tuple-element.27.refs_1_, bf16[6,3600,128]{2,1,0:T(8,128)(2,1)S(1)} %get-tuple-element.32.refs_2_, ...), custom_call_target="tpu_custom_call" | custom-call | flops 1000 | bytes 1000 | tf_op jit(solution)/shard_map/products/pallas_call | solution.py:290
  47.2 1.7 %collective-permute-start.6 = (bf16[16,3600]{1,0:T(8,128)(2,1)S(1)}, bf16[16,3600]{1,0:T(8,128)(2,1)S(1)}, u32[]{:S(2)}, u32[]{:S(2)}) collective-permute-start(bf16[16,3600]{1,0:T(8,128)(2,1)S(1)} %get-tuple-element.38.refs_8_), channel_id=1, source_target_pairs={{0,1},{1,2},{2,3},{4,5},{5,6},{6,7},{8,9},{9,10},{10,11},{12,13},{... | collective-permute-start | bytes 345608 | tf_op jit(solution)/shard_map/ppermute | solution.py:549
  48.9 1.3 %collective-permute-start.7 = (bf16[16,3600]{1,0:T(8,128)(2,1)S(1)}, bf16[16,3600]{1,0:T(8,128)(2,1)S(1)}, u32[]{:S(2)}, u32[]{:S(2)}) collective-permute-start(bf16[16,3600]{1,0:T(8,128)(2,1)S(1)} %get-tuple-element.39.refs_7_), channel_id=1, source_target_pairs={{1,0},{2,1},{3,2},{5,4},{6,5},{7,6},{9,8},{10,9},{11,10},{13,12},{... | collective-permute-start | bytes 345608 | tf_op jit(solution)/shard_map/ppermute | solution.py:554
  50.7 3.8 %collective-permute-done.7.refs_3_.refs_6_ = bf16[16,3600]{1,0:T(8,128)(2,1)S(1)} collective-permute-done((bf16[16,3600]{1,0:T(8,128)(2,1)S(1)}, bf16[16,3600]{1,0:T(8,128)(2,1)S(1)}, u32[]{:S(2)}, u32[]{:S(2)}) %collective-permute-start.7) | collective-permute-done | bytes 115232 | tf_op jit(solution)/shard_map/ppermute | solution.py:554
  55.1 2.3 %collective-permute-start.11 = (bf16[2,96,3600]{2,1,0:T(8,128)(2,1)S(1)}, bf16[2,96,3600]{2,1,0:T(8,128)(2,1)S(1)}, u32[]{:S(2)}, u32[]{:S(2)}) collective-permute-start(bf16[2,96,3600]{2,1,0:T(8,128)(2,1)S(1)} %get-tuple-element.45.refs_0_), channel_id=1, source_target_pairs={{0,16},{4,12},{8,24},{12,4},{16,0},{20,28},{24,8},{28,20},{1,17},{... | collective-permute-start | bytes 4147208 | tf_op jit(solution)/shard_map/ppermute | solution.py:479
  57.8 9.7 %average.1 = (bf16[8,3600,128]{2,1,0:T(8,128)(2,1)S(1)}, f32[8,128]{1,0:T(8,128)S(1)}) custom-call(bf16[3600,128]{1,0:T(8,128)(2,1)S(1)} %collective-permute-done.refs_0_, bf16[3600,128]{1,0:T(8,128)(2,1)S(1)} %get-tuple-element.27.refs_1_, bf16[6,3600,128]{2,1,0:T(8,128)(2,1)S(1)} %get-tuple-element.32.refs_2_, ...), custom_call_target="tpu_custom_call" | custom-call | flops 1000 | bytes 1000 | tf_op jit(solution)/shard_map/average/pallas_call | solution.py:395
  67.5 2.3 %score.4.best_ref = f32[2,4,8,8,128]{4,3,2,1,0:T(8,128)S(1)} custom-call(bf16[8,3600,128]{2,1,0:T(8,128)(2,1)S(1)} %get-tuple-element.43.a_ref, f32[2,4,8,8,128]{4,3,2,1,0:T(8,128)S(1)} %broadcast_in_dim.2.best_ref, bf16[2,64,3600]{2,1,0:T(8,128)(2,1)S(1)} %get-tuple-element.44.refs_0_, bf16[2,64,3600]{2,1,0:T(8,128)(2,1)S(1)} %collective-permute-done.9.refs_1_), custom_call_target="tpu_custom_call" | custom-call | flops 1000 | bytes 1000 | tf_op jit(solution)/shard_map/score/pallas_call | solution.py:466
  69.9 3.5 %score.5.refs_1_.best_ref = f32[2,4,8,8,128]{4,3,2,1,0:T(8,128)S(1)} custom-call(bf16[8,3600,128]{2,1,0:T(8,128)(2,1)S(1)} %get-tuple-element.43.a_ref, f32[2,4,8,8,128]{4,3,2,1,0:T(8,128)S(1)} %score.4.best_ref, bf16[2,96,3600]{2,1,0:T(8,128)(2,1)S(1)} %get-tuple-element.45.refs_0_, bf16[2,96,3600]{2,1,0:T(8,128)(2,1)S(1)} %collective-permute-done.10.refs_1_), custom_call_target="tpu_custom_call" | custom-call | flops 1000 | bytes 1000 | tf_op jit(solution)/shard_map/score/pallas_call | solution.py:466
  74.5 1.8 %score.6.best_ref = f32[2,4,8,8,128]{4,3,2,1,0:T(8,128)S(1)} custom-call(bf16[8,3600,128]{2,1,0:T(8,128)(2,1)S(1)} %get-tuple-element.43.a_ref, f32[2,4,8,8,128]{4,3,2,1,0:T(8,128)S(1)} %score.5.refs_1_.best_ref, bf16[2,96,3600]{2,1,0:T(8,128)(2,1)S(1)} %hold.1.refs_0_), custom_call_target="tpu_custom_call" | custom-call | flops 1000 | bytes 1000 | tf_op jit(solution)/shard_map/score/pallas_call | solution.py:466
  76.3 1.0 %collective-permute-done.12.refs_0_ = bf16[2,96,3600]{2,1,0:T(8,128)(2,1)S(1)} collective-permute-done((bf16[2,96,3600]{2,1,0:T(8,128)(2,1)S(1)}, bf16[2,96,3600]{2,1,0:T(8,128)(2,1)S(1)}, u32[]{:S(2)}, u32[]{:S(2)}) %collective-permute-start.12) | collective-permute-done | bytes 1382432 | tf_op jit(solution)/shard_map/ppermute | solution.py:479
  77.3 2.6 %score.7 = f32[2,4,8,128]{3,2,1,0:T(8,128)} custom-call(bf16[8,3600,128]{2,1,0:T(8,128)(2,1)S(1)} %get-tuple-element.43.a_ref, f32[2,4,8,8,128]{4,3,2,1,0:T(8,128)S(1)} %score.6.best_ref, bf16[2,96,3600]{2,1,0:T(8,128)(2,1)S(1)} %collective-permute-done.12.refs_0_, f32[8,128]{1,0:T(8,128)S(1)} %get-tuple-element.46.refs_1_), custom_call_target="tpu_custom_call" | custom-call | flops 1000 | bytes 1000 | tf_op jit(solution)/shard_map/score/pallas_call | solution.py:466
  (34 shorter events, 3.2 us)
Async XLA Ops:
  0.0 11.7 %copy-start = (bf16[2,16,3600]{2,1,0:T(8,128)(2,1)S(1)}, bf16[2,16,3600]{2,1,0:T(8,128)(2,1)}, u32[]{:S(2)}) copy-start(bf16[2,16,3600]{2,1,0:T(8,128)(2,1)} %refs_0_.3) | copy-start | bytes 691204
  0.0 11.7 %collective-permute-start.2 = (bf16[2,16,3600]{2,1,0:T(8,128)(2,1)}, bf16[2,16,3600]{2,1,0:T(8,128)(2,1)S(1)}, u32[]{:S(2)}, u32[]{:S(2)}) collective-permute-start(bf16[2,16,3600]{2,1,0:T(8,128)(2,1)} %refs_0_.3), channel_id=1, source_target_pairs={{0,8},{4,12},{8,0},{12,4},{16,24},{20,28},{24,16},{28,20},{1,9},{5... | collective-permute-start | bytes 691208 | tf_op jit(solution)/shard_map/ppermute | solution.py:479
  2.0 11.3 %collective-permute-start.1 = (bf16[2,16,3600]{2,1,0:T(8,128)(2,1)}, bf16[2,16,3600]{2,1,0:T(8,128)(2,1)S(1)}, u32[]{:S(2)}, u32[]{:S(2)}) collective-permute-start(bf16[2,16,3600]{2,1,0:T(8,128)(2,1)} %refs_0_.3), channel_id=1, source_target_pairs={{0,3},{1,2},{2,1},{3,0},{4,7},{5,6},{6,5},{7,4},{8,11},{9,10},{10,... | collective-permute-start | bytes 691208 | tf_op jit(solution)/shard_map/ppermute | solution.py:479
  12.1 18.5 %collective-permute-start.5 = (bf16[2,32,3600]{2,1,0:T(8,128)(2,1)S(1)}, bf16[2,32,3600]{2,1,0:T(8,128)(2,1)}, u32[]{:S(2)}, u32[]{:S(2)}) collective-permute-start(bf16[2,32,3600]{2,1,0:T(8,128)(2,1)S(1)} %get-tuple-element.34.refs_0_), channel_id=1, source_target_pairs={{0,16},{4,20},{8,24},{12,28},{16,0},{20,4},{24,8},{28,12},{1,17},{... | collective-permute-start | bytes 1382408 | tf_op jit(solution)/shard_map/ppermute | solution.py:479
  14.2 17.6 %collective-permute-start.4 = (bf16[2,32,3600]{2,1,0:T(8,128)(2,1)}, bf16[2,32,3600]{2,1,0:T(8,128)(2,1)}, u32[]{:S(2)}, u32[]{:S(2)}) collective-permute-start(bf16[2,32,3600]{2,1,0:T(8,128)(2,1)} %get-tuple-element.33), channel_id=1, source_target_pairs={{0,1},{1,0},{2,3},{3,2},{4,5},{5,4},{6,7},{7,6},{8,9},{9,8},{10,11... | collective-permute-start | bytes 1382408 | tf_op jit(solution)/shard_map/ppermute | solution.py:479
  16.3 18.2 %collective-permute-start = (bf16[3600,128]{1,0:T(8,128)(2,1)S(1)}, bf16[3600,128]{1,0:T(8,128)(2,1)S(1)}, u32[]{:S(2)}, u32[]{:S(2)}) collective-permute-start(bf16[3600,128]{1,0:T(8,128)(2,1)S(1)} %get-tuple-element.26.refs_3_), channel_id=1, source_target_pairs={{0,4},{4,8},{8,12},{12,16},{16,20},{20,24},{24,28},{1,5},{5,9},{9,... | collective-permute-start | bytes 2764808 | tf_op jit(solution)/shard_map/ppermute | solution.py:549
  20.0 23.0 %collective-permute-start.3 = (bf16[3600,128]{1,0:T(8,128)(2,1)S(1)}, bf16[3600,128]{1,0:T(8,128)(2,1)}, u32[]{:S(2)}, u32[]{:S(2)}) collective-permute-start(bf16[3600,128]{1,0:T(8,128)(2,1)S(1)} %get-tuple-element.27.refs_1_), channel_id=1, source_target_pairs={{4,0},{8,4},{12,8},{16,12},{20,16},{24,20},{28,24},{5,1},{9,5},{13... | collective-permute-start | bytes 2764808 | tf_op jit(solution)/shard_map/ppermute | solution.py:554
  33.0 21.5 %collective-permute-start.8 = (bf16[2,48,3600]{2,1,0:T(8,128)(2,1)S(1)}, bf16[2,48,3600]{2,1,0:T(8,128)(2,1)S(1)}, u32[]{:S(2)}, u32[]{:S(2)}) collective-permute-start(bf16[2,48,3600]{2,1,0:T(8,128)(2,1)S(1)} %get-tuple-element.41.refs_0_), channel_id=1, source_target_pairs={{0,8},{4,20},{8,0},{12,28},{16,24},{20,4},{24,16},{28,12},{1,9},{5... | collective-permute-start | bytes 2073608 | tf_op jit(solution)/shard_map/ppermute | solution.py:479
  47.2 10.6 %copy-start.1 = (s32[8,8,128]{2,1,0:T(8,128)S(1)}, s32[8,8,128]{2,1,0:T(8,128)}, u32[]{:S(2)}) copy-start(s32[8,8,128]{2,1,0:T(8,128)} %param.7) | copy-start | bytes 98308
  47.2 3.5 %collective-permute-start.6 = (bf16[16,3600]{1,0:T(8,128)(2,1)S(1)}, bf16[16,3600]{1,0:T(8,128)(2,1)S(1)}, u32[]{:S(2)}, u32[]{:S(2)}) collective-permute-start(bf16[16,3600]{1,0:T(8,128)(2,1)S(1)} %get-tuple-element.38.refs_8_), channel_id=1, source_target_pairs={{0,1},{1,2},{2,3},{4,5},{5,6},{6,7},{8,9},{9,10},{10,11},{12,13},{... | collective-permute-start | bytes 345608 | tf_op jit(solution)/shard_map/ppermute | solution.py:549
  48.9 5.6 %collective-permute-start.7 = (bf16[16,3600]{1,0:T(8,128)(2,1)S(1)}, bf16[16,3600]{1,0:T(8,128)(2,1)S(1)}, u32[]{:S(2)}, u32[]{:S(2)}) collective-permute-start(bf16[16,3600]{1,0:T(8,128)(2,1)S(1)} %get-tuple-element.39.refs_7_), channel_id=1, source_target_pairs={{1,0},{2,1},{3,2},{5,4},{6,5},{7,6},{9,8},{10,9},{11,10},{13,12},{... | collective-permute-start | bytes 345608 | tf_op jit(solution)/shard_map/ppermute | solution.py:554
  55.1 14.8 %collective-permute-start.10 = (bf16[2,96,3600]{2,1,0:T(8,128)(2,1)S(1)}, bf16[2,96,3600]{2,1,0:T(8,128)(2,1)S(1)}, u32[]{:S(2)}, u32[]{:S(2)}) collective-permute-start(bf16[2,96,3600]{2,1,0:T(8,128)(2,1)S(1)} %get-tuple-element.45.refs_0_), channel_id=1, source_target_pairs={{0,4},{4,0},{8,12},{12,8},{16,20},{20,16},{24,28},{28,24},{1,5},{5... | collective-permute-start | bytes 4147208 | tf_op jit(solution)/shard_map/ppermute | solution.py:479
  55.1 18.8 %collective-permute-start.11 = (bf16[2,96,3600]{2,1,0:T(8,128)(2,1)S(1)}, bf16[2,96,3600]{2,1,0:T(8,128)(2,1)S(1)}, u32[]{:S(2)}, u32[]{:S(2)}) collective-permute-start(bf16[2,96,3600]{2,1,0:T(8,128)(2,1)S(1)} %get-tuple-element.45.refs_0_), channel_id=1, source_target_pairs={{0,16},{4,12},{8,24},{12,4},{16,0},{20,28},{24,8},{28,20},{1,17},{... | collective-permute-start | bytes 4147208 | tf_op jit(solution)/shard_map/ppermute | solution.py:479
  57.5 10.0 %collective-permute-start.9 = (bf16[2,64,3600]{2,1,0:T(8,128)(2,1)S(1)}, bf16[2,64,3600]{2,1,0:T(8,128)(2,1)S(1)}, u32[]{:S(2)}, u32[]{:S(2)}) collective-permute-start(bf16[2,64,3600]{2,1,0:T(8,128)(2,1)S(1)} %get-tuple-element.44.refs_0_), channel_id=1, source_target_pairs={{0,4},{4,0},{8,12},{12,8},{16,20},{20,16},{24,28},{28,24},{1,5},{5... | collective-permute-start | bytes 2764808 | tf_op jit(solution)/shard_map/ppermute | solution.py:479
  73.9 3.4 %collective-permute-start.12 = (bf16[2,96,3600]{2,1,0:T(8,128)(2,1)S(1)}, bf16[2,96,3600]{2,1,0:T(8,128)(2,1)S(1)}, u32[]{:S(2)}, u32[]{:S(2)}) collective-permute-start(bf16[2,96,3600]{2,1,0:T(8,128)(2,1)S(1)} %hold.1.refs_0_), channel_id=1, source_target_pairs={{0,4},{4,0},{8,12},{12,8},{16,20},{20,16},{24,28},{28,24},{1,5},{5... | collective-permute-start | bytes 4147208 | tf_op jit(solution)/shard_map/ppermute | solution.py:479

commit v3 on v2

--- a/solution.py
+++ b/solution.py
@@ -17,6 +17,7 @@
 CHUNK = GROUPS * TILE
 DEPTH = 256
 LANES = 128
+SLOTS = 6
 SIDES = 32
 
 epsilon = 1e-05
@@ -70,16 +71,16 @@
     ref[...] = jnp.zeros(ref.shape, ref.dtype)
 
 
-def standard_rows(both, mat_ref, half, corr, sq, stores):
+def standard_rows(both, mat_ref, work, corr, stores):
     for g in range(GROUPS):
         rhs = tiles_of([both(quad, slice(g * TILE, (g + 1) * TILE)) for quad in range(GROUPS)])
         out = jnp.dot(mat_ref[0], rhs, preferred_element_type=jnp.float32)
-        half[g] = out.astype(jnp.bfloat16)
+        work[g] = out.astype(jnp.bfloat16)
 
     total = jnp.zeros((8, 2 * LANES), jnp.float32)
     squares = jnp.zeros((8, 2 * LANES), jnp.float32)
     for quad in range(GROUPS):
-        rhs = tiles_of([half[g, pl.ds(quad * TILE, TILE), :] for g in range(GROUPS)])
+        rhs = tiles_of([work[g, pl.ds(quad * TILE, TILE), :] for g in range(GROUPS)])
         background = jnp.dot(mat_ref[1], rhs, preferred_element_type=jnp.float32)
         corrected = both(quad, slice(None)).astype(jnp.float32) - background
         corr[quad] = corrected
@@ -91,26 +92,27 @@
     variance = jnp.sum(squares, axis=0, keepdims=True) / pixels - mean * mean
     scale = 1.0 / jnp.sqrt(jnp.maximum(variance, 0.0) + epsilon)
     for quad in range(GROUPS):
-        sq[quad] = ((corr[quad] - mean) * scale).astype(jnp.bfloat16)
+        work[quad] = ((corr[quad] - mean) * scale).astype(jnp.bfloat16)
     for g in range(GROUPS):
-        rhs = tiles_of([sq[quad, pl.ds(g * TILE, TILE), :] for quad in range(GROUPS)])
+        rhs = tiles_of([work[quad, pl.ds(g * TILE, TILE), :] for quad in range(GROUPS)])
         out = jnp.dot(mat_ref[2], rhs, preferred_element_type=jnp.float32).astype(jnp.bfloat16)
         for side, store in enumerate(stores):
             store(slice(g * CHUNK, (g + 1) * CHUNK), out[:, side * LANES : (side + 1) * LANES])
 
 
-def border_kernel(x_hbm, mask_hbm, mat_hbm, xq_hbm, first, last, token, mask_ref, mat_ref, xq, ends, raw, half, corr, sq, sems):
-    rows = raw.shape[2]
+def border_kernel(x_hbm, mask_hbm, mat_hbm, xq_hbm, first, last, token, mask_ref, mat_ref, xq, ends, raw, work, corr, sems):
+    rows, slots = raw.shape[2], raw.shape[0]
     mark(token)
 
     def fetch(g):
-        return pltpu.make_async_copy(x_hbm.at[pl.ds(g * CHUNK, CHUNK)], raw.at[g], sems.at[g])
-
-    mask_copy = pltpu.make_async_copy(mask_hbm, mask_ref, sems.at[GROUPS])
-    matrices = pltpu.make_async_copy(mat_hbm, mat_ref, sems.at[GROUPS + 1])
-    keep = pltpu.make_async_copy(xq, xq_hbm, sems.at[GROUPS + 2])
+        slot = g % slots
+        return pltpu.make_async_copy(x_hbm.at[pl.ds(g * CHUNK, CHUNK)], raw.at[slot], sems.at[slot])
+
+    mask_copy = pltpu.make_async_copy(mask_hbm, mask_ref, sems.at[slots])
+    matrices = pltpu.make_async_copy(mat_hbm, mat_ref, sems.at[slots + 1])
+    keep = pltpu.make_async_copy(xq, xq_hbm, sems.at[slots + 2])
     mask_copy.start()
-    for g in range(GROUPS):
+    for g in range(slots):
         fetch(g).start()
     matrices.start()
     mask_copy.wait()
@@ -119,13 +121,15 @@
         fetch(g).wait()
         for quad in range(GROUPS):
             piece = jnp.concatenate(
-                [raw[g, pl.ds(row * PH + quad * QUAD, QUAD)] for row in range(QUAD)], axis=0
+                [raw[g % slots, pl.ds(row * PH + quad * QUAD, QUAD)] for row in range(QUAD)], axis=0
             )
             tile = jnp.swapaxes(piece * mask, 0, 1)
             span = slice(g * TILE, (g + 1) * TILE)
             xq[:, quad, span, :] = tile[1 : rows - 1]
             ends[0, quad, span, :] = tile[0]
             ends[1, quad, span, :] = tile[rows - 1]
+        if g + slots < GROUPS:
+            fetch(g + slots).start()
     keep.start()
     matrices.wait()
 
@@ -138,7 +142,7 @@
 
         return put
 
-    standard_rows(both, mat_ref, half, corr, sq, [store(first), store(last)])
+    standard_rows(both, mat_ref, work, corr, [store(first), store(last)])
     keep.wait()
 
 
@@ -146,7 +150,6 @@
     return [
         pltpu.VMEM((GROUPS, CHUNK, 2 * cols), jnp.bfloat16),
         pltpu.VMEM((GROUPS, CHUNK, 2 * cols), jnp.float32),
-        pltpu.VMEM((GROUPS, CHUNK, 2 * cols), jnp.bfloat16),
     ]
 
 
@@ -168,18 +171,18 @@
             pltpu.VMEM(matrices.shape, bf16),
             pltpu.VMEM((rows - 2, GROUPS, CHUNK, cols), bf16),
             pltpu.VMEM((2, GROUPS, CHUNK, cols), bf16),
-            pltpu.VMEM((GROUPS, CHUNK, rows, cols), bf16),
+            pltpu.VMEM((SLOTS, CHUNK, rows, cols), bf16),
         ]
         + row_scratch(cols)
-        + [pltpu.SemaphoreType.DMA((GROUPS + 3,))],
-        compiler_params=pltpu.CompilerParams(vmem_limit_bytes=26 * MIB),
+        + [pltpu.SemaphoreType.DMA((SLOTS + 3,))],
+        compiler_params=pltpu.CompilerParams(vmem_limit_bytes=18 * MIB),
         cost_estimate=SHORT,
         name="border",
     )(in_hbm(patterns), in_hbm(scan_mask), in_hbm(matrices))
 
 
 def interior_kernel(xq_hbm, mat_hbm, *refs):
-    s_ref, token, mat_ref, xq, half, corr, sq, sems = refs[-8:]
+    s_ref, token, mat_ref, xq, buffer, corr, sems = refs[-7:]
     mark(token)
     pairs = s_ref.shape[0] // 2
     matrices = pltpu.make_async_copy(mat_hbm, mat_ref, sems.at[2])
@@ -204,7 +207,7 @@
 
             return put
 
-        standard_rows(both, mat_ref, half, corr, sq, [store(0), store(1)])
+        standard_rows(both, mat_ref, buffer, corr, [store(0), store(1)])
 
     for i in range(pairs):
         fetch(i).wait()
@@ -218,7 +221,7 @@
     pixels = GROUPS * CHUNK
     return pl.pallas_call(
         interior_kernel,
-        in_specs=[APART, APART] + [WHOLE] * len(earlier),
+        in_specs=[APART, APART] + [APART] * len(earlier),
         out_specs=(WHOLE, WHOLE),
         out_shape=(pltpu.VMEM((rows, pixels, cols), jnp.bfloat16), TOKEN),
         scratch_shapes=[
@@ -227,7 +230,7 @@
         ]
         + row_scratch(cols)
         + [pltpu.SemaphoreType.DMA((3,))],
-        compiler_params=pltpu.CompilerParams(vmem_limit_bytes=16 * MIB),
+        compiler_params=pltpu.CompilerParams(vmem_limit_bytes=11 * MIB),
         cost_estimate=SHORT,
         name="interior",
     )(in_hbm(xq), in_hbm(matrices), *earlier)
@@ -242,6 +245,28 @@
         return {-1: above, 0: first, rows - 1: last, rows: below}[r]
 
     return row
+
+
+def fetch_halo(refs, halo, sems):
+    copies = [
+        pltpu.make_async_copy(refs[0], halo.at[0], sems.at[0]),
+        pltpu.make_async_copy(refs[4], halo.at[1], sems.at[1]),
+    ]
+    for copy in copies:
+        copy.start()
+    return (halo.at[0], refs[1], refs[2], refs[3], halo.at[1]), [copy.wait for copy in copies]
+
+
+HALO = pl.BlockSpec(memory_space=pl.ANY)
+BLOCK = [HALO, WHOLE, WHOLE, WHOLE, HALO]
+
+
+def halo_scratch(pixels, cols):
+    return [pltpu.VMEM((2, pixels, cols), jnp.bfloat16), pltpu.SemaphoreType.DMA((2,))]
+
+
+def on_chip_but_halo(block):
+    return [block[0], *map(on_chip, block[1:4]), block[4]]
 
 
 def diagonals(product, at_sub, at_lane):
@@ -255,19 +280,24 @@
 
 
 def products_kernel(*refs):
-    left, right, out = refs[-3:]
+    left, right, out, halo, sems = refs[-5:]
     rows = refs[2].shape[0] + 2
-    row = row_of(refs[:5], rows)
-    cols = refs[0].shape[1]
+    cols = refs[1].shape[1]
+    block, waits = fetch_halo(refs[:5], halo, sems)
+    row = row_of(block, rows)
     f32 = jnp.float32
     at_sub = lax.broadcasted_iota(jnp.int32, (cols, cols), 0)
     at_lane = lax.broadcasted_iota(jnp.int32, (cols, cols), 1)
-    firsts, lasts = [], []
-    for r in range(-1, rows + 1):
+    firsts, lasts = {}, {}
+    for r in [*range(rows - 1), rows - 1, rows, -1]:
+        if r == rows - 1:
+            waits[1]()
+        if r == -1:
+            waits[0]()
         here = row(r)[...]
         across = here.T
-        firsts.append(across[:1])
-        lasts.append(across[cols - 1 :])
+        firsts[r] = across[:1]
+        lasts[r] = across[cols - 1 :]
         pieces = [here]
         if r < rows:
             pieces.append(row(r + 1)[...])
@@ -278,9 +308,10 @@
             vectors += diagonals(product[:, cols:], at_sub, at_lane)
         vectors += [jnp.zeros((1, cols), f32)] * (PER_ROW - len(vectors))
         out[r + 1] = jnp.concatenate(vectors, axis=0)
-    blank = [jnp.zeros((SIDES // 2 - len(firsts), here.shape[0]), firsts[0].dtype)]
-    left[...] = jnp.concatenate(firsts + blank, axis=0)
-    right[...] = jnp.concatenate(lasts + blank, axis=0)
+    blank = [jnp.zeros((SIDES // 2 - len(firsts), here.shape[0]), here.dtype)]
+    order = range(-1, rows + 1)
+    left[...] = jnp.concatenate([firsts[r] for r in order] + blank, axis=0)
+    right[...] = jnp.concatenate([lasts[r] for r in order] + blank, axis=0)
 
 
 def products(block, *earlier):
@@ -289,20 +320,22 @@
     one = jax.ShapeDtypeStruct((SIDES // 2, pixels), jnp.bfloat16)
     return pl.pallas_call(
         products_kernel,
-        in_specs=[WHOLE] * (5 + len(earlier)),
+        in_specs=BLOCK + [APART] * len(earlier),
         out_specs=(WHOLE,) * 3,
         out_shape=(one, one, jax.ShapeDtypeStruct((rows + 2, PER_ROW, cols), jnp.float32)),
-        compiler_params=pltpu.CompilerParams(vmem_limit_bytes=12 * MIB),
+        scratch_shapes=halo_scratch(pixels, cols),
+        compiler_params=pltpu.CompilerParams(vmem_limit_bytes=6 * MIB),
         cost_estimate=SHORT,
         name="products",
-    )(*map(on_chip, block), *earlier)
+    )(*on_chip_but_halo(block), *earlier)
 
 
 def average_kernel(*refs):
     left_ref, right_ref, own_left_ref, own_right_ref, dot_ref, usable_ref = refs[5:11]
-    a_ref, inv_ref, sides, weights = refs[-4:]
+    a_ref, inv_ref, sides, weights, halo, sems = refs[-6:]
     rows, pixels, cols = a_ref.shape
-    row = row_of(refs[:5], rows)
+    block, waits = fetch_halo(refs[:5], halo, sems)
+    row = row_of(block, rows)
     f32 = jnp.float32
     at_sub = lax.broadcasted_iota(jnp.int32, (cols, cols), 0)
     at_lane = lax.broadcasted_iota(jnp.int32, (cols, cols), 1)
@@ -330,7 +363,11 @@
     def kept(r, k):
         return dot_ref[r + 1, pl.ds(k, 1), :]
 
-    for r in range(rows):
+    for r in [*range(1, rows - 1), 0, rows - 1]:
+        if r == 0:
+            waits[0]()
+        if r == rows - 1:
+            waits[1]()
         weight = {}
         slot = 0
         total = jnp.ones((1, cols), f32)
@@ -394,7 +431,7 @@
     pixels, cols = block[0].shape
     return pl.pallas_call(
         average_kernel,
-        in_specs=[WHOLE] * (11 + len(earlier)),
+        in_specs=BLOCK + [WHOLE] * 6 + [APART] * len(earlier),
         out_specs=(WHOLE, WHOLE),
         out_shape=(
             pltpu.VMEM((rows, pixels, cols), jnp.bfloat16),
@@ -403,11 +440,12 @@
         scratch_shapes=[
             pltpu.VMEM((pixels, cols), jnp.bfloat16),
             pltpu.VMEM((4, cols, cols), jnp.float32),
-        ],
-        compiler_params=pltpu.CompilerParams(vmem_limit_bytes=8 * MIB),
+        ]
+        + halo_scratch(pixels, cols),
+        compiler_params=pltpu.CompilerParams(vmem_limit_bytes=6 * MIB),
         cost_estimate=SHORT,
         name="average",
-    )(*map(on_chip, block), left, right, own_left, own_right, dots, usable, *earlier)
+    )(*on_chip_but_halo(block), left, right, own_left, own_right, dots, usable, *earlier)
 
 
 def insert(best, new):
@@ -462,16 +500,16 @@
     last = [] if inv_pattern is None else [inv_pattern]
     panels, top, rows, sublanes, cols = best.shape
     shape = (panels, top, rows, cols) if last else best.shape
-    out = jax.ShapeDtypeStruct(shape, jnp.float32)
+    out = jax.ShapeDtypeStruct(shape, jnp.float32) if last else pltpu.VMEM(shape, jnp.float32)
     return pl.pallas_call(
         functools.partial(score_kernel, len(pieces)),
         in_specs=[WHOLE] * (2 + len(pieces) + len(last)),
         out_specs=WHOLE,
         out_shape=out,
-        compiler_params=pltpu.CompilerParams(vmem_limit_bytes=14 * MIB),
+        compiler_params=pltpu.CompilerParams(vmem_limit_bytes=2 * MIB),
         cost_estimate=SHORT,
         name="score",
-    )(on_chip(averaged), best, *pieces, *last)
+    )(on_chip(averaged), on_chip(best), *pieces, *last)
 
 
 def exchange(x, axis, masks):
@@ -489,11 +527,11 @@
 
     return pl.pallas_call(
         nothing,
-        in_specs=[APART] + [WHOLE] * len(earlier),
+        in_specs=[APART] + [APART] * len(earlier),
         out_specs=APART,
         out_shape=jax.ShapeDtypeStruct(x.shape, x.dtype),
         input_output_aliases={0: 0},
-        compiler_params=pltpu.CompilerParams(vmem_limit_bytes=MIB),
+        compiler_params=pltpu.CompilerParams(vmem_limit_bytes=MIB // 8),
         cost_estimate=SHORT,
         name="hold",
     )(x, *earlier)
@@ -521,11 +559,11 @@
     size = sum(part.shape[1] for part in parts)
     return pl.pallas_call(
         functools.partial(join_kernel, len(parts)),
-        in_specs=[APART] * len(parts) + [WHOLE] * len(earlier),
+        in_specs=[APART] * len(parts) + [APART] * len(earlier),
         out_specs=(APART, WHOLE),
         out_shape=(jax.ShapeDtypeStruct((panels, size, pixels), parts[0].dtype), TOKEN),
         scratch_shapes=[pltpu.SemaphoreType.DMA((len(parts),))],
-        compiler_params=pltpu.CompilerParams(vmem_limit_bytes=MIB),
+        compiler_params=pltpu.CompilerParams(vmem_limit_bytes=MIB // 8),
         cost_estimate=SHORT,
         name="join",
     )(*parts, *earlier)
@@ -583,50 +621,43 @@
         near = held = dictionary
         mirrored, *masks = line_masks(line)
         far = [exchange(held, "dict", (mirrored, mirrored))]
-        plain = [(even, even) for even, _ in ways]
-        near_new = exchange(near, "strip", plain[0])
+        near_new = exchange(near, "strip", ways[0])
 
     xq, first, last, bordered = border(patterns, scan_mask, matrices)
     above = from_low(last, "strip")
     below = from_high(first, "strip")
-    joined = [bordered]
+    middle, filled = interior(xq, matrices, bordered)
+    block = (above, first, middle, last, below)
     if not alone:
         for mask in masks:
-            held, done = join([held, far[-1]], bordered)
+            held, _ = join([held, far[-1]], filled)
             far.append(exchange(held, "dict", (mask, mask)))
-            joined.append(done)
-        for way in plain[1:]:
-            near, done = join([near, near_new], bordered)
-            near_new = exchange(near, "strip", way)
-            joined.append(done)
-
-    middle, filled = interior(xq, matrices, *joined)
-    block = (above, first, middle, last, below)
-    joined = [filled]
-    if not alone:
-        near, done = join([near, near_new], filled)
-        near_other = exchange(near, "strip", (1, 1))
-        far, done = join(far, done)
-        far_new = exchange(far, "strip", ways[0])
-        joined = [done]
-
-    own_left, own_right, dots = products(block, *joined)
+
+    own_left, own_right, dots = products(block)
     left = from_low(own_right, "dict")
     right = from_high(own_left, "dict")
     joined = []
     if not alone:
+        far, done = join(far, dots)
+        far_new = exchange(far, "strip", ways[0])
         for way in ways[1:]:
             far, done = join([far, far_new], left, right)
             far_new = exchange(far, "strip", way)
         joined = [done]
-        far_other = exchange(far, "strip", (1, 1))
+        for way in ways[1:]:
+            near, done = join([near, near_new], done)
+            near_new = exchange(near, "strip", way)
+        joined.append(done)
 
     averaged, inv_pattern = average(block, left, right, own_left, own_right, dots, usable, *joined)
     if alone:
         whole = lax.all_gather(dictionary, ("strip", "dict"), axis=1, tiled=True)
         return score(averaged, best, [whole], inv_pattern)
+    near, _ = join([near, near_new], inv_pattern)
+    near_other = exchange(near, "strip", (1, 1))
+    far_other = exchange(far, "strip", (1, 1))
+    best = score(averaged, best, [far, far_other])
     best = score(averaged, best, [near, near_other])
-    best = score(averaged, best, [far, far_other])
     far_new = hold(far_new, best)
     far_new_other = exchange(far_new, "strip", (1, 1))
     best = score(averaged, best, [far_new])

time: 80.6 us -> 92 us (1.14)
  waiting for transfers between devices: 14.3 us -> 30.9 us
  starting transfers between devices: 21.8 us -> 16.8 us
    ppermute x9, waiting for transfers between devices: 1.54 us -> 15.3 us  [exchange(): return lax.ppermute(x, axis, [(i, i ^ masks[i & 1]) for i in range(count)])]
    ppermute x9, starting transfers between devices: 13 us -> 8.64 us  [exchange(): return lax.ppermute(x, axis, [(i, i ^ masks[i & 1]) for i in range(count)])]
    ppermute x2, waiting for transfers between devices: 12.3 us -> 14.9 us  [from_high(): return lax.ppermute(x, axis, [(i + 1, i) for i in range(count - 1)])]
  transfers between devices with their start and end apart: 13 -> 13, of which waited for: 5 -> 6; matrix products, arithmetic and copies ran while one was open for 1% -> 1% of each run, Pallas kernels for 50% -> 44%
where the time goes in v3:
time: 92 us; the launch traced here: 91.7 us
  Pallas kernels  43 us (47%)
  waiting for transfers between devices  30.9 us (34%)
  starting transfers between devices  16.8 us (18%)
    ppermute x9, waiting for transfers between devices, exchange(): return lax.ppermute(x, axis, [(i, i ^ masks[i & 1]) for i in range(count)])  15.3 us
    ppermute x2, waiting for transfers between devices, from_high(): return lax.ppermute(x, axis, [(i + 1, i) for i in range(count - 1)])  14.9 us
    pallas_call x4, Pallas kernels, score(): pl.pallas_call(functools.partial(score_kernel, len(pieces)), in_specs=[WH...  10.2 us
    pallas_call x1, Pallas kernels, average(): pl.pallas_call(average_kernel, in_specs=BLOCK + [WHOLE] * 6 + [APART] * l...  9.52 us
    ppermute x9, starting transfers between devices, exchange(): return lax.ppermute(x, axis, [(i, i ^ masks[i & 1]) for i in range(count)])  8.64 us
    pallas_call x1, Pallas kernels, interior(): pl.pallas_call(interior_kernel, in_specs=[APART, APART] + [APART] * len(e...  8.39 us
    pallas_call x1, Pallas kernels, border(): pl.pallas_call(border_kernel, in_specs=[APART] * 3, out_specs=(APART, WHO...  6.72 us
    ppermute x2, starting transfers between devices, from_low(): return lax.ppermute(x, axis, [(i, i + 1) for i in range(count - 1)])  4.54 us
  transfers between devices with their start and end apart: 13, of which 6 were waited for; matrix products, arithmetic and copies ran while one was open for 1% of the time, Pallas kernels for 44%

profile of v3, /device:TPU:1, one launch (start us, length us, event | category | flops | bytes accessed | tf_op | source)
XLA Modules:
  0.0 91.7 jit_solution(14267921916098207108)
XLA Ops:
  0.0 4.2 %collective-permute-start.4 = (bf16[2,16,3600]{2,1,0:T(8,128)(2,1)}, bf16[2,16,3600]{2,1,0:T(8,128)(2,1)S(1)}, u32[]{:S(2)}, u32[]{:S(2)}) collective-permute-start(bf16[2,16,3600]{2,1,0:T(8,128)(2,1)} %refs_0_.3), channel_id=1, source_target_pairs={{0,3},{1,2},{2,1},{3,0},{4,7},{5,6},{6,5},{7,4},{8,11},{9,10},{10,... | collective-permute-start | bytes 691208 | tf_op jit(solution)/shard_map/ppermute | solution.py:517
  4.2 1.2 %collective-permute-start.7 = (bf16[2,16,3600]{2,1,0:T(8,128)(2,1)}, bf16[2,16,3600]{2,1,0:T(8,128)(2,1)S(1)}, u32[]{:S(2)}, u32[]{:S(2)}) collective-permute-start(bf16[2,16,3600]{2,1,0:T(8,128)(2,1)} %refs_0_.3), channel_id=1, source_target_pairs={{0,8},{4,20},{8,0},{12,28},{16,24},{20,4},{24,16},{28,12},{1,9},{5... | collective-permute-start | bytes 691208 | tf_op jit(solution)/shard_map/ppermute | solution.py:517
  5.4 6.7 %border.1 = (bf16[6,15,240,128]{3,2,1,0:T(8,128)(2,1)}, bf16[3600,128]{1,0:T(8,128)(2,1)S(1)}, bf16[3600,128]{1,0:T(8,128)(2,1)S(1)}, f32[8,128]{1,0:T(8,128)S(1)}) custom-call(bf16[3600,8,128]{2,1,0:T(8,128)(2,1)} %x_hbm.1, s32[8,128]{1,0:T(8,128)} %mask_hbm.1, bf16[3,240,256]{2,1,0:T(8,128)(2,1)} %constant.11.clone.mat_hbm), custom_call_target="tpu_custom_call" | custom-call | flops 1000 | bytes 1000 | tf_op jit(solution)/shard_map/border/pallas_call | solution.py:159
  12.1 3.3 %collective-permute-start = (bf16[3600,128]{1,0:T(8,128)(2,1)S(1)}, bf16[3600,128]{1,0:T(8,128)(2,1)S(1)}, u32[]{:S(2)}, u32[]{:S(2)}) collective-permute-start(bf16[3600,128]{1,0:T(8,128)(2,1)S(1)} %get-tuple-element.23.refs_3_), channel_id=1, source_target_pairs={{0,4},{4,8},{8,12},{12,16},{16,20},{20,24},{24,28},{1,5},{5,9},{9,... | collective-permute-start | bytes 2764808 | tf_op jit(solution)/shard_map/ppermute | solution.py:587
  15.4 2.1 %collective-permute-start.1 = (bf16[3600,128]{1,0:T(8,128)(2,1)S(1)}, bf16[3600,128]{1,0:T(8,128)(2,1)}, u32[]{:S(2)}, u32[]{:S(2)}) collective-permute-start(bf16[3600,128]{1,0:T(8,128)(2,1)S(1)} %get-tuple-element.24.refs_1_), channel_id=1, source_target_pairs={{4,0},{8,4},{12,8},{16,12},{20,16},{24,20},{28,24},{5,1},{9,5},{13... | collective-permute-start | bytes 2764808 | tf_op jit(solution)/shard_map/ppermute | solution.py:592
  17.5 8.4 %interior.1 = (bf16[6,3600,128]{2,1,0:T(8,128)(2,1)S(1)}, f32[8,128]{1,0:T(8,128)S(1)}) custom-call(bf16[6,15,240,128]{3,2,1,0:T(8,128)(2,1)} %get-tuple-element.25.xq_hbm, bf16[3,240,256]{2,1,0:T(8,128)(2,1)} %constant.11.clone.mat_hbm, f32[8,128]{1,0:T(8,128)S(1)} %get-tuple-element.26.refs_0_), custom_call_target="tpu_custom_call" | custom-call | flops 1000 | bytes 1000 | tf_op jit(solution)/shard_map/interior/pallas_call | solution.py:222
  26.0 0.9 join.5
  27.2 11.1 %collective-permute-done.1.refs_4_ = bf16[3600,128]{1,0:T(8,128)(2,1)} collective-permute-done((bf16[3600,128]{1,0:T(8,128)(2,1)S(1)}, bf16[3600,128]{1,0:T(8,128)(2,1)}, u32[]{:S(2)}, u32[]{:S(2)}) %collective-permute-start.1) | collective-permute-done | bytes 921632 | tf_op jit(solution)/shard_map/ppermute | solution.py:592
  38.3 4.4 %products.1 = (bf16[16,3600]{1,0:T(8,128)(2,1)S(1)}, bf16[16,3600]{1,0:T(8,128)(2,1)S(1)}, f32[10,8,128]{2,1,0:T(8,128)S(1)}) custom-call(bf16[3600,128]{1,0:T(8,128)(2,1)S(1)} %collective-permute-done.refs_0_, bf16[3600,128]{1,0:T(8,128)(2,1)S(1)} %get-tuple-element.24.refs_1_, bf16[6,3600,128]{2,1,0:T(8,128)(2,1)S(1)} %get-tuple-element.27.refs_2_, ...), custom_call_target="tpu_custom_call" | custom-call | flops 1000 | bytes 1000 | tf_op jit(solution)/shard_map/products/pallas_call | solution.py:321
  42.8 0.9 %join.6 = (bf16[2,48,3600]{2,1,0:T(8,128)(2,1)S(1)}, f32[8,128]{1,0:T(8,128)}) custom-call(bf16[2,16,3600]{2,1,0:T(8,128)(2,1)S(1)} %collective-permute-done.4.refs_1_.refs_0_, bf16[2,32,3600]{2,1,0:T(8,128)(2,1)S(1)} %collective-permute-done.5.refs_1_, f32[10,8,128]{2,1,0:T(8,128)S(1)} %get-tuple-element.30.refs_2_.refs_9_), custom_call_target="tpu_custom_call" | custom-call | flops 1000 | bytes 1000 | tf_op jit(solution)/shard_map/join/pallas_call | solution.py:560
  44.0 1.3 %collective-permute-start.2 = (bf16[16,3600]{1,0:T(8,128)(2,1)S(1)}, bf16[16,3600]{1,0:T(8,128)(2,1)S(1)}, u32[]{:S(2)}, u32[]{:S(2)}) collective-permute-start(bf16[16,3600]{1,0:T(8,128)(2,1)S(1)} %get-tuple-element.28.refs_8_), channel_id=1, source_target_pairs={{0,1},{1,2},{2,3},{4,5},{5,6},{6,7},{8,9},{9,10},{10,11},{12,13},{... | collective-permute-start | bytes 345608 | tf_op jit(solution)/shard_map/ppermute | solution.py:587
  45.3 1.5 %collective-permute-start.3 = (bf16[16,3600]{1,0:T(8,128)(2,1)S(1)}, bf16[16,3600]{1,0:T(8,128)(2,1)S(1)}, u32[]{:S(2)}, u32[]{:S(2)}) collective-permute-start(bf16[16,3600]{1,0:T(8,128)(2,1)S(1)} %get-tuple-element.29.refs_7_), channel_id=1, source_target_pairs={{1,0},{2,1},{3,2},{5,4},{6,5},{7,6},{9,8},{10,9},{11,10},{13,12},{... | collective-permute-start | bytes 345608 | tf_op jit(solution)/shard_map/ppermute | solution.py:592
  47.6 3.8 %collective-permute-done.3.refs_3_.refs_6_ = bf16[16,3600]{1,0:T(8,128)(2,1)S(1)} collective-permute-done((bf16[16,3600]{1,0:T(8,128)(2,1)S(1)}, bf16[16,3600]{1,0:T(8,128)(2,1)S(1)}, u32[]{:S(2)}, u32[]{:S(2)}) %collective-permute-start.3) | collective-permute-done | bytes 115232 | tf_op jit(solution)/shard_map/ppermute | solution.py:592
  51.4 2.4 %collective-permute-done.6.refs_1_ = bf16[2,48,3600]{2,1,0:T(8,128)(2,1)S(1)} collective-permute-done((bf16[2,48,3600]{2,1,0:T(8,128)(2,1)S(1)}, bf16[2,48,3600]{2,1,0:T(8,128)(2,1)S(1)}, u32[]{:S(2)}, u32[]{:S(2)}) %collective-permute-start.6) | collective-permute-done | bytes 691232 | tf_op jit(solution)/shard_map/ppermute | solution.py:517
  54.3 1.0 %collective-permute-start.11 = (bf16[2,96,3600]{2,1,0:T(8,128)(2,1)S(1)}, bf16[2,96,3600]{2,1,0:T(8,128)(2,1)S(1)}, u32[]{:S(2)}, u32[]{:S(2)}) collective-permute-start(bf16[2,96,3600]{2,1,0:T(8,128)(2,1)S(1)} %get-tuple-element.37.refs_0_), channel_id=1, source_target_pairs={{0,16},{4,12},{8,24},{12,4},{16,0},{20,28},{24,8},{28,20},{1,17},{... | collective-permute-start | bytes 4147208 | tf_op jit(solution)/shard_map/ppermute | solution.py:517
  56.4 9.5 %average.1 = (bf16[8,3600,128]{2,1,0:T(8,128)(2,1)S(1)}, f32[8,128]{1,0:T(8,128)S(1)}) custom-call(bf16[3600,128]{1,0:T(8,128)(2,1)S(1)} %collective-permute-done.refs_0_, bf16[3600,128]{1,0:T(8,128)(2,1)S(1)} %get-tuple-element.24.refs_1_, bf16[6,3600,128]{2,1,0:T(8,128)(2,1)S(1)} %get-tuple-element.27.refs_2_, ...), custom_call_target="tpu_custom_call" | custom-call | flops 1000 | bytes 1000 | tf_op jit(solution)/shard_map/average/pallas_call | solution.py:432
  65.9 11.5 %collective-permute-done.9.refs_1_ = bf16[2,32,3600]{2,1,0:T(8,128)(2,1)S(1)} collective-permute-done((bf16[2,32,3600]{2,1,0:T(8,128)(2,1)S(1)}, bf16[2,32,3600]{2,1,0:T(8,128)(2,1)S(1)}, u32[]{:S(2)}, u32[]{:S(2)}) %collective-permute-start.9) | collective-permute-done | bytes 460832 | tf_op jit(solution)/shard_map/ppermute | solution.py:517
  77.4 1.2 %join.9 = (bf16[2,64,3600]{2,1,0:T(8,128)(2,1)S(1)}, f32[8,128]{1,0:T(8,128)}) custom-call(bf16[2,32,3600]{2,1,0:T(8,128)(2,1)S(1)} %get-tuple-element.38.refs_0_, bf16[2,32,3600]{2,1,0:T(8,128)(2,1)S(1)} %collective-permute-done.9.refs_1_, f32[8,128]{1,0:T(8,128)S(1)} %get-tuple-element.39.refs_2_.refs_1_), custom_call_target="tpu_custom_call" | custom-call | flops 1000 | bytes 1000 | tf_op jit(solution)/shard_map/join/pallas_call | solution.py:560
  78.6 1.4 %collective-permute-start.10 = (bf16[2,64,3600]{2,1,0:T(8,128)(2,1)S(1)}, bf16[2,64,3600]{2,1,0:T(8,128)(2,1)S(1)}, u32[]{:S(2)}, u32[]{:S(2)}) collective-permute-start(bf16[2,64,3600]{2,1,0:T(8,128)(2,1)S(1)} %get-tuple-element.40.refs_0_), channel_id=1, source_target_pairs={{0,4},{4,0},{8,12},{12,8},{16,20},{20,16},{24,28},{28,24},{1,5},{5... | collective-permute-start | bytes 2764808 | tf_op jit(solution)/shard_map/ppermute | solution.py:517
  80.0 3.5 %score.4.best_ref = f32[2,4,8,8,128]{4,3,2,1,0:T(8,128)S(1)} custom-call(bf16[8,3600,128]{2,1,0:T(8,128)(2,1)S(1)} %get-tuple-element.36.a_ref, f32[2,4,8,8,128]{4,3,2,1,0:T(8,128)S(1)} %broadcast_in_dim.2.best_ref, bf16[2,96,3600]{2,1,0:T(8,128)(2,1)S(1)} %get-tuple-element.37.refs_0_, bf16[2,96,3600]{2,1,0:T(8,128)(2,1)S(1)} %collective-permute-done.8.refs_1_), custom_call_target="tpu_custom_call" | custom-call | flops 1000 | bytes 1000 | tf_op jit(solution)/shard_map/score/pallas_call | solution.py:504
  83.5 2.4 %score.5.refs_1_.best_ref = f32[2,4,8,8,128]{4,3,2,1,0:T(8,128)S(1)} custom-call(bf16[8,3600,128]{2,1,0:T(8,128)(2,1)S(1)} %get-tuple-element.36.a_ref, f32[2,4,8,8,128]{4,3,2,1,0:T(8,128)S(1)} %score.4.best_ref, bf16[2,64,3600]{2,1,0:T(8,128)(2,1)S(1)} %get-tuple-element.40.refs_0_, bf16[2,64,3600]{2,1,0:T(8,128)(2,1)S(1)} %collective-permute-done.10.refs_1_), custom_call_target="tpu_custom_call" | custom-call | flops 1000 | bytes 1000 | tf_op jit(solution)/shard_map/score/pallas_call | solution.py:504
  85.9 1.8 %score.6.best_ref = f32[2,4,8,8,128]{4,3,2,1,0:T(8,128)S(1)} custom-call(bf16[8,3600,128]{2,1,0:T(8,128)(2,1)S(1)} %get-tuple-element.36.a_ref, f32[2,4,8,8,128]{4,3,2,1,0:T(8,128)S(1)} %score.5.refs_1_.best_ref, bf16[2,96,3600]{2,1,0:T(8,128)(2,1)S(1)} %hold.1.refs_0_), custom_call_target="tpu_custom_call" | custom-call | flops 1000 | bytes 1000 | tf_op jit(solution)/shard_map/score/pallas_call | solution.py:504
  87.8 1.3 %collective-permute-done.12.refs_0_ = bf16[2,96,3600]{2,1,0:T(8,128)(2,1)S(1)} collective-permute-done((bf16[2,96,3600]{2,1,0:T(8,128)(2,1)S(1)}, bf16[2,96,3600]{2,1,0:T(8,128)(2,1)S(1)}, u32[]{:S(2)}, u32[]{:S(2)}) %collective-permute-start.12) | collective-permute-done | bytes 1382432 | tf_op jit(solution)/shard_map/ppermute | solution.py:517
  89.1 2.6 %score.7 = f32[2,4,8,128]{3,2,1,0:T(8,128)} custom-call(bf16[8,3600,128]{2,1,0:T(8,128)(2,1)S(1)} %get-tuple-element.36.a_ref, f32[2,4,8,8,128]{4,3,2,1,0:T(8,128)S(1)} %score.6.best_ref, bf16[2,96,3600]{2,1,0:T(8,128)(2,1)S(1)} %collective-permute-done.12.refs_0_, f32[8,128]{1,0:T(8,128)S(1)} %get-tuple-element.39.refs_2_.refs_1_), custom_call_target="tpu_custom_call" | custom-call | flops 1000 | bytes 1000 | tf_op jit(solution)/shard_map/score/pallas_call | solution.py:504
  (34 shorter events, 3.0 us)
Async XLA Ops:
  0.0 26.0 %collective-permute-start.4 = (bf16[2,16,3600]{2,1,0:T(8,128)(2,1)}, bf16[2,16,3600]{2,1,0:T(8,128)(2,1)S(1)}, u32[]{:S(2)}, u32[]{:S(2)}) collective-permute-start(bf16[2,16,3600]{2,1,0:T(8,128)(2,1)} %refs_0_.3), channel_id=1, source_target_pairs={{0,3},{1,2},{2,1},{3,0},{4,7},{5,6},{6,5},{7,4},{8,11},{9,10},{10,... | collective-permute-start | bytes 691208 | tf_op jit(solution)/shard_map/ppermute | solution.py:517
  4.2 51.1 %collective-permute-start.7 = (bf16[2,16,3600]{2,1,0:T(8,128)(2,1)}, bf16[2,16,3600]{2,1,0:T(8,128)(2,1)S(1)}, u32[]{:S(2)}, u32[]{:S(2)}) collective-permute-start(bf16[2,16,3600]{2,1,0:T(8,128)(2,1)} %refs_0_.3), channel_id=1, source_target_pairs={{0,8},{4,20},{8,0},{12,28},{16,24},{20,4},{24,16},{28,12},{1,9},{5... | collective-permute-start | bytes 691208 | tf_op jit(solution)/shard_map/ppermute | solution.py:517
  12.1 15.1 %collective-permute-start = (bf16[3600,128]{1,0:T(8,128)(2,1)S(1)}, bf16[3600,128]{1,0:T(8,128)(2,1)S(1)}, u32[]{:S(2)}, u32[]{:S(2)}) collective-permute-start(bf16[3600,128]{1,0:T(8,128)(2,1)S(1)} %get-tuple-element.23.refs_3_), channel_id=1, source_target_pairs={{0,4},{4,8},{8,12},{12,16},{16,20},{20,24},{24,28},{1,5},{5,9},{9,... | collective-permute-start | bytes 2764808 | tf_op jit(solution)/shard_map/ppermute | solution.py:587
  15.4 22.9 %collective-permute-start.1 = (bf16[3600,128]{1,0:T(8,128)(2,1)S(1)}, bf16[3600,128]{1,0:T(8,128)(2,1)}, u32[]{:S(2)}, u32[]{:S(2)}) collective-permute-start(bf16[3600,128]{1,0:T(8,128)(2,1)S(1)} %get-tuple-element.24.refs_1_), channel_id=1, source_target_pairs={{4,0},{8,4},{12,8},{16,12},{20,16},{24,20},{28,24},{5,1},{9,5},{13... | collective-permute-start | bytes 2764808 | tf_op jit(solution)/shard_map/ppermute | solution.py:592
  17.5 8.5 %copy-start = (bf16[2,16,3600]{2,1,0:T(8,128)(2,1)S(1)}, bf16[2,16,3600]{2,1,0:T(8,128)(2,1)}, u32[]{:S(2)}) copy-start(bf16[2,16,3600]{2,1,0:T(8,128)(2,1)} %refs_0_.3) | copy-start | bytes 691204
  26.9 15.8 %collective-permute-start.5 = (bf16[2,32,3600]{2,1,0:T(8,128)(2,1)S(1)}, bf16[2,32,3600]{2,1,0:T(8,128)(2,1)S(1)}, u32[]{:S(2)}, u32[]{:S(2)}) collective-permute-start(bf16[2,32,3600]{2,1,0:T(8,128)(2,1)S(1)} %get-tuple-element.32), channel_id=1, source_target_pairs={{0,1},{1,0},{2,3},{3,2},{4,5},{5,4},{6,7},{7,6},{8,9},{9,8},{10,11... | collective-permute-start | bytes 1382408 | tf_op jit(solution)/shard_map/ppermute | solution.py:517
  42.8 13.6 %copy-start.1 = (s32[8,8,128]{2,1,0:T(8,128)S(1)}, s32[8,8,128]{2,1,0:T(8,128)}, u32[]{:S(2)}) copy-start(s32[8,8,128]{2,1,0:T(8,128)} %param.7) | copy-start | bytes 98308
  43.7 10.1 %collective-permute-start.6 = (bf16[2,48,3600]{2,1,0:T(8,128)(2,1)S(1)}, bf16[2,48,3600]{2,1,0:T(8,128)(2,1)S(1)}, u32[]{:S(2)}, u32[]{:S(2)}) collective-permute-start(bf16[2,48,3600]{2,1,0:T(8,128)(2,1)S(1)} %get-tuple-element.33.refs_0_), channel_id=1, source_target_pairs={{0,8},{4,20},{8,0},{12,28},{16,24},{20,4},{24,16},{28,12},{1,9},{5... | collective-permute-start | bytes 2073608 | tf_op jit(solution)/shard_map/ppermute | solution.py:517
  44.0 3.7 %collective-permute-start.2 = (bf16[16,3600]{1,0:T(8,128)(2,1)S(1)}, bf16[16,3600]{1,0:T(8,128)(2,1)S(1)}, u32[]{:S(2)}, u32[]{:S(2)}) collective-permute-start(bf16[16,3600]{1,0:T(8,128)(2,1)S(1)} %get-tuple-element.28.refs_8_), channel_id=1, source_target_pairs={{0,1},{1,2},{2,3},{4,5},{5,6},{6,7},{8,9},{9,10},{10,11},{12,13},{... | collective-permute-start | bytes 345608 | tf_op jit(solution)/shard_map/ppermute | solution.py:587
  45.3 6.2 %collective-permute-start.3 = (bf16[16,3600]{1,0:T(8,128)(2,1)S(1)}, bf16[16,3600]{1,0:T(8,128)(2,1)S(1)}, u32[]{:S(2)}, u32[]{:S(2)}) collective-permute-start(bf16[16,3600]{1,0:T(8,128)(2,1)S(1)} %get-tuple-element.29.refs_7_), channel_id=1, source_target_pairs={{1,0},{2,1},{3,2},{5,4},{6,5},{7,6},{9,8},{10,9},{11,10},{13,12},{... | collective-permute-start | bytes 345608 | tf_op jit(solution)/shard_map/ppermute | solution.py:592
  54.2 25.8 %collective-permute-start.8 = (bf16[2,96,3600]{2,1,0:T(8,128)(2,1)S(1)}, bf16[2,96,3600]{2,1,0:T(8,128)(2,1)S(1)}, u32[]{:S(2)}, u32[]{:S(2)}) collective-permute-start(bf16[2,96,3600]{2,1,0:T(8,128)(2,1)S(1)} %get-tuple-element.37.refs_0_), channel_id=1, source_target_pairs={{0,4},{4,0},{8,12},{12,8},{16,20},{20,16},{24,28},{28,24},{1,5},{5... | collective-permute-start | bytes 4147208 | tf_op jit(solution)/shard_map/ppermute | solution.py:517
  54.3 31.6 %collective-permute-start.11 = (bf16[2,96,3600]{2,1,0:T(8,128)(2,1)S(1)}, bf16[2,96,3600]{2,1,0:T(8,128)(2,1)S(1)}, u32[]{:S(2)}, u32[]{:S(2)}) collective-permute-start(bf16[2,96,3600]{2,1,0:T(8,128)(2,1)S(1)} %get-tuple-element.37.refs_0_), channel_id=1, source_target_pairs={{0,16},{4,12},{8,24},{12,4},{16,0},{20,28},{24,8},{28,20},{1,17},{... | collective-permute-start | bytes 4147208 | tf_op jit(solution)/shard_map/ppermute | solution.py:517
  55.6 21.8 %collective-permute-start.9 = (bf16[2,32,3600]{2,1,0:T(8,128)(2,1)S(1)}, bf16[2,32,3600]{2,1,0:T(8,128)(2,1)S(1)}, u32[]{:S(2)}, u32[]{:S(2)}) collective-permute-start(bf16[2,32,3600]{2,1,0:T(8,128)(2,1)S(1)} %get-tuple-element.38.refs_0_), channel_id=1, source_target_pairs={{0,16},{4,12},{8,24},{12,4},{16,0},{20,28},{24,8},{28,20},{1,17},{... | collective-permute-start | bytes 1382408 | tf_op jit(solution)/shard_map/ppermute | solution.py:517
  78.6 4.9 %collective-permute-start.10 = (bf16[2,64,3600]{2,1,0:T(8,128)(2,1)S(1)}, bf16[2,64,3600]{2,1,0:T(8,128)(2,1)S(1)}, u32[]{:S(2)}, u32[]{:S(2)}) collective-permute-start(bf16[2,64,3600]{2,1,0:T(8,128)(2,1)S(1)} %get-tuple-element.40.refs_0_), channel_id=1, source_target_pairs={{0,4},{4,0},{8,12},{12,8},{16,20},{20,16},{24,28},{28,24},{1,5},{5... | collective-permute-start | bytes 2764808 | tf_op jit(solution)/shard_map/ppermute | solution.py:517
  85.8 3.3 %collective-permute-start.12 = (bf16[2,96,3600]{2,1,0:T(8,128)(2,1)S(1)}, bf16[2,96,3600]{2,1,0:T(8,128)(2,1)S(1)}, u32[]{:S(2)}, u32[]{:S(2)}) collective-permute-start(bf16[2,96,3600]{2,1,0:T(8,128)(2,1)S(1)} %hold.1.refs_0_), channel_id=1, source_target_pairs={{0,4},{4,0},{8,12},{12,8},{16,20},{20,16},{24,28},{28,24},{1,5},{5... | collective-permute-start | bytes 4147208 | tf_op jit(solution)/shard_map/ppermute | solution.py:517
